TPU v7x, 32 devices: a whole 2x2x4 slice. The times are simulated.
32 devices in a mesh: groups: 2 (over x), tm: 16 (over z, y, core).
Axes of the slice: x: 2, y: 2, z: 4, core: 2. Of those that a mesh axis runs over, the one named last changes fastest.
Arguments:
- tokens: bfloat16 [4096, 1536], P(('groups', 'tm')), parts along dimension 0, may hold values from -6 to 6
- target: bfloat16 [4096, 1536], P(('groups', 'tm')), parts along dimension 0, may hold values from -3 to 3
- w_query: bfloat16 [1536, 1536], P('tm'), may hold values from -0.15625 to 0.15625
- w_key: bfloat16 [1536, 1536], P('tm'), may hold values from -0.15625 to 0.15625
- w_value: bfloat16 [1536, 1536], P('tm'), may hold values from -0.15625 to 0.15625
- q_gain: float32 [128], replicated, may hold values from 0.5 to 2
- k_gain: float32 [128], replicated, may hold values from 0.5 to 2
- block_weight: float32 [16], P('groups'), parts along dimension 0
- block_reset: int32 [16], P('groups'), parts along dimension 0, may hold values 0 or 1
- valid_count: int32 [16], P('groups'), parts along dimension 0, may hold values from 192 to 256
Outputs:
- input_grad: bfloat16 [4096, 1536], P(('groups', 'tm')), parts along dimension 0
- loss: float32 [2], P('groups'), parts along dimension 0
There are 2 independent parts, one for each index of `groups`. A program takes and returns all parts, laid end to end along the dimension named above; an argument that names none is the same for every part. Nothing has to cross between parts.
All inputs are finite; a program needn't handle non-finite values.
Results may differ from a plain program's by a relative error of at most 0.012.
The roundings to bfloat16 on the way count: a program that leaves them out, or rounds other values in their place, can miss the bound.
Values may be sent and summed in bfloat16 or wider, within the bound.
A program may use at most 128 MiB of HBM per device.

v0:
```python
import math

import jax
import jax.numpy as jnp
from jax import lax
from jax.sharding import PartitionSpec as P

epsilon = 1e-06
loss_scale = 32.0
group_heads = 4


def swapped(value, axis, stride):
    mask = 2**stride
    pairs = [(source, source ^ mask) for source in range(lax.axis_size(axis))]
    return lax.ppermute(value, axis, pairs)


def from_behind(block, axis, distance):
    devices = range(lax.axis_size(axis))
    route = [(i - distance, i) for i in devices if i - distance in devices]
    return lax.ppermute(block, axis, route)


def unit_heads(values, head_size):
    shaped = values.reshape(values.shape[0], values.shape[1] // head_size, head_size)
    factor = lax.rsqrt(jnp.mean(shaped * shaped, axis=-1, keepdims=True) + epsilon)
    return (shaped * factor, factor)


def norm_backward(upstream, unit, factor, gain):
    shaped = upstream.reshape(unit.shape) * gain
    result = factor * (shaped - unit * jnp.mean(shaped * unit, axis=-1, keepdims=True))
    return result.reshape(upstream.shape)


def pick_entry(table, position):
    marks = jnp.arange(table.shape[0], dtype=jnp.int32) == position
    return jnp.sum(jnp.where(marks, table, jnp.zeros_like(table)))


def back_project(grad, weight):
    return lax.dot_general(
        grad, weight, (((1,), (1,)), ((), ())), preferred_element_type=jnp.float32
    )


def group_pass(query_part, key_part, value_part, allowed, row_weight, target_part, head_size):
    query_rows = query_part.shape[0]
    key_rows = key_part.shape[0]
    heads = query_part.shape[1] // head_size
    query_heads = query_part.reshape(query_rows, heads, head_size)
    key_heads = key_part.reshape(key_rows, heads, head_size)
    value_heads = value_part.reshape(key_rows, heads, head_size)
    scores = jnp.einsum(
        "qhd,khd->hqk", query_heads, key_heads, preferred_element_type=jnp.float32
    ) / math.sqrt(head_size)
    expo = jnp.where(allowed[None, None, :], jnp.exp(scores), jnp.zeros_like(scores))
    probs = expo / jnp.sum(expo, axis=-1, keepdims=True)
    probs_cast = probs.astype(jnp.bfloat16)
    attended = jnp.einsum(
        "hqk,khd->qhd", probs_cast, value_heads, preferred_element_type=jnp.float32
    )
    attended = attended.reshape(query_rows, heads * head_size).astype(jnp.bfloat16)
    diff = attended.astype(jnp.float32) - target_part.astype(jnp.float32)
    loss_part = jnp.sum(row_weight[:, None] * diff * diff)
    attended_grad = (loss_scale * row_weight[:, None] * diff).astype(jnp.bfloat16)
    grad_heads = attended_grad.reshape(query_rows, heads, head_size)
    prob_grad = jnp.einsum(
        "qhd,khd->hqk", grad_heads, value_heads, preferred_element_type=jnp.float32
    )
    delta = jnp.sum(probs * prob_grad, axis=-1, keepdims=True)
    score_grad = (probs * (prob_grad - delta) / math.sqrt(head_size)).astype(jnp.bfloat16)
    value_grad = jnp.einsum(
        "hqk,qhd->khd", probs_cast, grad_heads, preferred_element_type=jnp.float32
    ).reshape(key_rows, heads * head_size)
    query_grad = jnp.einsum(
        "hqk,khd->qhd", score_grad, key_heads, preferred_element_type=jnp.float32
    ).reshape(query_rows, heads * head_size)
    key_grad = jnp.einsum(
        "hqk,qhd->khd", score_grad, query_heads, preferred_element_type=jnp.float32
    ).reshape(key_rows, heads * head_size)
    return (loss_part, query_grad, key_grad, value_grad)


def per_device(
    tokens, target, w_query, w_key, w_value, q_gain, k_gain, block_weight, block_reset, valid_count
):
    row_count = tokens.shape[0]
    head_size = q_gain.shape[0]
    block_len = 2 * row_count
    place = lax.axis_index("tm")
    parity = place % 2
    block_index = place // 2
    full_query, full_key, full_value = (
        lax.all_gather(w_query, "tm", axis=0, tiled=True),
        lax.all_gather(w_key, "tm", axis=0, tiled=True),
        lax.all_gather(w_value, "tm", axis=0, tiled=True),
    )
    keys_raw = jnp.dot(tokens, full_key, preferred_element_type=jnp.float32)
    values_raw = jnp.dot(tokens, full_value, preferred_element_type=jnp.float32)
    key_unit, key_factor = unit_heads(keys_raw, head_size)
    key_normed = (key_unit * k_gain).reshape(keys_raw.shape).astype(jnp.bfloat16)
    key_unit, key_factor, key_normed, value_cast = (
        key_unit,
        key_factor,
        key_normed,
        values_raw.astype(jnp.bfloat16),
    )
    queries_raw = jnp.dot(tokens, full_query, preferred_element_type=jnp.float32)
    query_unit, query_factor = unit_heads(queries_raw, head_size)
    query_normed = (query_unit * q_gain).reshape(queries_raw.shape).astype(jnp.bfloat16)
    query_unit, query_factor, query_normed = (query_unit, query_factor, query_normed)
    partner_key, partner_value = swapped((key_normed, value_cast), "tm", 0)
    is_first = parity == 0
    own_keys = jnp.concatenate(
        [
            jnp.where(is_first, key_normed, partner_key),
            jnp.where(is_first, partner_key, key_normed),
        ],
        axis=0,
    )
    own_values = jnp.concatenate(
        [
            jnp.where(is_first, value_cast, partner_value),
            jnp.where(is_first, partner_value, value_cast),
        ],
        axis=0,
    )
    earlier_keys, earlier_values = from_behind((own_keys, own_values), "tm", 2)
    all_keys = jnp.concatenate([earlier_keys, own_keys], axis=0)
    all_values = jnp.concatenate([earlier_values, own_values], axis=0)
    own_count = pick_entry(valid_count, block_index)
    prior_count = pick_entry(valid_count, block_index - 1)
    reset_flag = pick_entry(block_reset, block_index)
    key_place = jnp.arange(2 * block_len, dtype=jnp.int32)
    in_own = key_place >= block_len
    key_pos = key_place % block_len
    limit = jnp.where(in_own, own_count, prior_count)
    allowed = (key_pos < limit) & (in_own | (block_index > 0) & (reset_flag == 0))
    query_pos = parity * row_count + jnp.arange(row_count, dtype=jnp.int32)
    row_weight = jnp.where(query_pos < own_count, pick_entry(block_weight, block_index), 0.0)
    width = query_normed.shape[1]
    group_width = group_heads * head_size
    loss_part = jnp.zeros((), jnp.float32)
    query_grads, key_grads, value_grads = ([], [], [])
    for group in range(width // group_width):
        start = group * group_width
        stop = start + group_width
        part_loss, query_grad, key_grad, value_grad = group_pass(
            query_normed[:, start:stop],
            all_keys[:, start:stop],
            all_values[:, start:stop],
            allowed,
            row_weight,
            target[:, start:stop],
            head_size,
        )
        loss_part = loss_part + part_loss
        query_grads.append(query_grad)
        key_grads.append(key_grad)
        value_grads.append(value_grad)
    query_grad = jnp.concatenate(query_grads, axis=1)
    key_grad = jnp.concatenate(key_grads, axis=1)
    value_grad = jnp.concatenate(value_grads, axis=1)
    loss_sum = lax.psum(loss_part, "tm")
    mine_start = parity * row_count
    other_start = (1 - parity) * row_count
    back_key, back_value = from_behind((key_grad[:block_len], value_grad[:block_len]), "tm", -2)
    pair_key = key_grad[block_len:] + back_key
    pair_value = value_grad[block_len:] + back_value
    mine_key = lax.dynamic_slice_in_dim(pair_key, mine_start, row_count, 0)
    mine_value = lax.dynamic_slice_in_dim(pair_value, mine_start, row_count, 0)
    other_key = lax.dynamic_slice_in_dim(pair_key, other_start, row_count, 0)
    other_value = lax.dynamic_slice_in_dim(pair_value, other_start, row_count, 0)
    given_key, given_value = swapped((other_key, other_value), "tm", 0)
    total_key = mine_key + given_key
    total_value = mine_value + given_value
    query_back = norm_backward(query_grad, query_unit, query_factor, q_gain).astype(jnp.bfloat16)
    key_back = norm_backward(total_key, key_unit, key_factor, k_gain).astype(jnp.bfloat16)
    value_back = total_value.astype(jnp.bfloat16)
    input_grad = (
        back_project(query_back, full_query)
        + back_project(key_back, full_key)
        + back_project(value_back, full_value)
    )
    loss = (loss_sum / (row_count * lax.axis_size("tm") * width)).reshape(1)
    return (input_grad.astype(jnp.bfloat16), loss)


def solution(mesh):
    return jax.shard_map(
        per_device,
        mesh=mesh,
        in_specs=(
            P(("groups", "tm"), None),
            P(("groups", "tm"), None),
            P("tm", None),
            P("tm", None),
            P("tm", None),
            P(),
            P(),
            P("groups"),
            P("groups"),
            P("groups"),
        ),
        out_specs=(P(("groups", "tm"), None), P("groups")),
        check_vma=False,
    )
```

profile of v0, /device:TPU:0, one launch (start us, length us, event | category | flops | bytes accessed | tf_op | source)
XLA Modules:
  0.0 385.3 jit_solution(3084836586877436594)
XLA Ops:
  9.4 1.4 select_reduce_fusion.2
  11.5 1.9 fusion.87
  13.4 1.3 select_reduce_fusion
  14.6 1.9 broadcast_multiply_fusion.2
  17.1 1.2 broadcast_bitcast_fusion.1
  18.4 48.0 %all-gather.4.cloned.1.call-done = bf16[1536,1536]{1,0:T(8,128)(2,1)} async-done(((bf16[96,1536]{1,0:T(8,128)(2,1)}), bf16[1536,1536]{1,0:T(8,128)(2,1)}) %all-gather.4.cloned.1.call-update) | async-done | bytes 4718608 | tf_op jit(solution)/shard_map/all_gather | solution.py:96
  66.4 3.1 fusion.116
  70.3 50.4 %all-gather.6.cloned.1.call-done = bf16[1536,1536]{1,0:T(8,128)(2,1)} async-done(((bf16[96,1536]{1,0:T(8,128)(2,1)}), bf16[1536,1536]{1,0:T(8,128)(2,1)}) %all-gather.6.cloned.1.call-update) | async-done | bytes 4718608 | tf_op jit(solution)/shard_map/all_gather | solution.py:97
  120.7 3.1 fusion.117
  124.2 1.1 mul.212
  125.3 2.3 copy.50
  127.5 2.3 multiply_convert_fusion.3
  130.1 44.8 %all-gather.8.cloned.1.call-done = bf16[1536,1536]{1,0:T(8,128)(2,1)} async-done(((bf16[96,1536]{1,0:T(8,128)(2,1)}), bf16[1536,1536]{1,0:T(8,128)(2,1)}) %all-gather.8.cloned.1.call-update) | async-done | bytes 4718608 | tf_op jit(solution)/shard_map/all_gather | solution.py:98
  174.9 3.1 convolution_convert_fusion
  178.4 1.0 multiply_convert_fusion.2
  179.4 1.1 broadcast_select_fusion.3
  180.5 3.3 collective-permute-start.1
  184.3 1.1 broadcast_select_fusion.1
  185.4 1.0 pad_maximum_fusion.5
  186.4 4.5 %collective-permute-start.3 = (bf16[256,1536]{1,0:T(8,128)(2,1)}, bf16[256,1536]{1,0:T(8,128)(2,1)}, u32[]{:S(2)}, u32[]{:S(2)}) collective-permute-start(bf16[256,1536]{1,0:T(8,128)(2,1)} %pad_maximum_fusion.5), channel_id=1, source_target_pairs={{0,2},{1,3},{2,4},{3,5},{4,6},{5,7},{6,8},{7,9},{8,10},{9,11},{10,... | collective-permute-start | bytes 2359304 | tf_op jit(solution)/shard_map/ppermute | solution.py:22
  190.8 10.0 %collective-permute-done.1 = bf16[256,1536]{1,0:T(8,128)(2,1)} collective-permute-done((bf16[256,1536]{1,0:T(8,128)(2,1)S(1)}, bf16[256,1536]{1,0:T(8,128)(2,1)}, u32[]{:S(2)}, u32[]{:S(2)}) %collective-permute-start.1) | collective-permute-done | bytes 786464 | tf_op jit(solution)/shard_map/ppermute | solution.py:22
  200.9 1.2 pad_maximum_fusion.2
  202.5 1.5 fusion.50
  203.9 1.4 fusion.14
  205.8 1.4 fusion.16
  207.2 1.5 fusion.52
  209.1 1.6 fusion.54
  210.7 6.5 %collective-permute-done.3 = bf16[256,1536]{1,0:T(8,128)(2,1)} collective-permute-done((bf16[256,1536]{1,0:T(8,128)(2,1)}, bf16[256,1536]{1,0:T(8,128)(2,1)}, u32[]{:S(2)}, u32[]{:S(2)}) %collective-permute-start.3) | collective-permute-done | bytes 786464 | tf_op jit(solution)/shard_map/ppermute | solution.py:22
  217.2 1.2 pad_maximum_fusion.3
  218.7 2.0 fusion.22
  220.8 2.8 fusion.23
  223.6 1.1 copy.62
  224.7 1.1 fusion.24
  225.8 1.1 copy.55
  226.9 2.5 fusion.72
  230.0 3.3 fusion.73
  233.3 1.3 fusion.44
  234.7 3.0 fusion.76
  237.8 1.4 fusion.47
  239.2 2.9 fusion.79
  242.1 2.0 fusion.35
  244.4 2.6 fusion.30
  247.4 2.8 fusion.25
  250.1 1.3 copy.88
  251.5 1.4 pad_maximum_fusion
  252.9 1.3 slice.74
  254.2 1.5 collective-permute-start.4
  256.8 1.3 slice.76
  258.1 1.4 collective-permute-start.6
  261.4 2.9 convolution_bitcast_fusion
  264.3 3.5 convolution_bitcast_fusion.1
  267.9 3.7 convolution_bitcast_fusion.2
  271.6 2.3 pad_maximum_fusion.6
  273.9 76.1 %psum.7 = f32[]{:T(128)} all-reduce(f32[]{:T(128)S(6)} %add.94), channel_id=1, replica_groups=mesh['groups'=2,'tm'=16] {'tm'}, use_global_device_ids=true, to_apply=%region_17.18 | all-reduce | flops 1 | bytes 8 | tf_op jit(solution)/shard_map/psum | solution.py:166
  350.0 1.0 mul.241
  351.0 2.3 copy.74
  353.3 2.3 copy.73
  356.3 6.0 %fusion.67 = f32[128,1536]{1,0:T(8,128)} fusion(bf16[1536,1536]{1,0:T(8,128)(2,1)} %all-gather.4.cloned.1.call-done, f32[128,1536]{1,0:T(8,128)} %copy-done.6, f32[128,1536]{1,0:T(8,128)} %get-tuple-element.10, f32[128,1536]{1,0:T(8,128)} %copy.74, f32[128,1536]{1,0:T(8,128)} %copy.73, f32[1536]{0:T(1024)S(1)} %broadcast_bitcast_fusion), kind=kOutput, calls=%fused_computation.98 | convolution fusion | flops 604962816 | bytes 8656896 | tf_op jit(solution)/shard_map/dot_general | solution.py:43
  362.3 1.6 slice_add_fusion.1
  364.1 1.7 slice_add_fusion
  365.8 1.0 constant_dynamic-slice_fusion
  368.0 1.2 copy.83
  369.2 4.8 %convolution_add_fusion.1 = f32[128,1536]{1,0:T(8,128)S(1)} fusion(f32[128,1536]{1,0:T(8,128)} %fusion.67, bf16[1536,1536]{1,0:T(8,128)(2,1)} %all-gather.6.cloned.1.call-done, f32[128,1536]{1,0:T(8,128)S(1)} %copy-done.8, f32[128,1536]{1,0:T(8,128)} %get-tuple-element.12, f32[128,1536]{1,0:T(8,128)} %copy.83, f32[128,1536]{1,0:T(8,128)S(1)} %dynamic-slice_add_fusion, ...), kind=kOutput, calls=%fused_computation.6 | convolution fusion | flops 605159424 | bytes 9443328 | tf_op jit(solution)/shard_map/dot_general | solution.py:43
  374.0 3.6 fusion.3
  (112 shorter events, 10.1 us)
Async XLA Ops:
  7.2 59.3 %copy-start = (bf16[128,1536]{1,0:T(8,128)(2,1)S(1)}, bf16[128,1536]{1,0:T(8,128)(2,1)}, u32[]{:S(2)}) copy-start(bf16[128,1536]{1,0:T(8,128)(2,1)} %param.10) | copy-start | bytes 1179652
  7.2 59.2 %all-gather.4.cloned.1.call-start = ((), (), s32[]{:S(2)}) async-start(), calls=%async_computation | async-start | bytes 5013504 | tf_op jit(solution)/shard_map/all_gather | solution.py:96
  7.9 112.8 %all-gather.6.cloned.1.call-start = ((), (), s32[]{:S(2)}) async-start(), calls=%async_computation.1 | async-start | bytes 5013504 | tf_op jit(solution)/shard_map/all_gather | solution.py:97
  8.7 166.3 %all-gather.8.cloned.1.call-start = ((), (), s32[]{:S(2)}) async-start(), calls=%async_computation.2 | async-start | bytes 5013504 | tf_op jit(solution)/shard_map/all_gather | solution.py:98
  69.8 50.9 %copy-start.7 = (f32[128,1536]{0,1:T(8,128)}, f32[128,1536]{0,1:T(8,128)S(1)}, u32[]{:S(2)}) copy-start(f32[128,1536]{0,1:T(8,128)S(1)} %copy.48) | copy-start | bytes 2359300
  69.9 53.9 %copy-start.22 = (f32[128,12]{0,1:T(8,128)}, f32[128,12]{0,1:T(8,128)S(1)}, u32[]{:S(2)}) copy-start(f32[128,12]{0,1:T(8,128)S(1)} %add_rsqrt_fusion.1) | copy-start | bytes 18436
  70.3 108.1 %copy-start.6 = (f32[128,1536]{1,0:T(8,128)}, f32[128,1536]{1,0:T(8,128)S(1)}, u32[]{:S(2)}) copy-start(f32[128,1536]{1,0:T(8,128)S(1)} %copy.75) | copy-start | bytes 2359300
  124.1 54.0 %copy-start.4 = (f32[128,1536]{0,1:T(8,128)}, f32[128,1536]{0,1:T(8,128)S(1)}, u32[]{:S(2)}) copy-start(f32[128,1536]{0,1:T(8,128)S(1)} %copy.49) | copy-start | bytes 2359300
  129.8 49.6 %collective-permute-start = (bf16[128,1536]{1,0:T(8,128)(2,1)}, bf16[128,1536]{1,0:T(8,128)(2,1)S(1)}, u32[]{:S(2)}, u32[]{:S(2)}) collective-permute-start(bf16[128,1536]{1,0:T(8,128)(2,1)} %get-tuple-element.11), channel_id=1, source_target_pairs={{0,1},{1,0},{2,3},{3,2},{4,5},{5,4},{6,7},{7,6},{8,9},{9,8},{10,11... | collective-permute-start | bytes 1179656 | tf_op jit(solution)/shard_map/ppermute | solution.py:16
  178.1 6.2 %collective-permute-start.2 = (bf16[128,1536]{1,0:T(8,128)(2,1)S(1)}, bf16[128,1536]{1,0:T(8,128)(2,1)}, u32[]{:S(2)}, u32[]{:S(2)}) collective-permute-start(bf16[128,1536]{1,0:T(8,128)(2,1)S(1)} %convolution_convert_fusion), channel_id=1, source_target_pairs={{0,1},{1,0},{2,3},{3,2},{4,5},{5,4},{6,7},{7,6},{8,9},{9,8},{10,11... | collective-permute-start | bytes 1179656 | tf_op jit(solution)/shard_map/ppermute | solution.py:16
  180.5 20.3 %collective-permute-start.1 = (bf16[256,1536]{1,0:T(8,128)(2,1)S(1)}, bf16[256,1536]{1,0:T(8,128)(2,1)}, u32[]{:S(2)}, u32[]{:S(2)}) collective-permute-start(bf16[256,1536]{1,0:T(8,128)(2,1)S(1)} %pad_maximum_fusion.4), channel_id=1, source_target_pairs={{0,2},{1,3},{2,4},{3,5},{4,6},{5,7},{6,8},{7,9},{8,10},{9,11},{10,... | collective-permute-start | bytes 2359304 | tf_op jit(solution)/shard_map/ppermute | solution.py:22
  184.3 24.8 %copy-start.15 = (bf16[128,512]{0,1:T(8,128)(2,1)}, bf16[128,512]{0,1:T(8,128)(2,1)S(1)}, u32[]{:S(2)}) copy-start(bf16[128,512]{0,1:T(8,128)(2,1)S(1)} %copy.92) | copy-start | bytes 393220
  186.4 16.1 %copy-start.25 = (pred[512]{0:T(512)(128)(4,1)S(1)}, pred[512]{0:T(512)(128)(4,1)}, u32[]{:S(2)}) copy-start(pred[512]{0:T(512)(128)(4,1)} %fusion.87) | copy-start | bytes 1540
  186.4 30.8 %collective-permute-start.3 = (bf16[256,1536]{1,0:T(8,128)(2,1)}, bf16[256,1536]{1,0:T(8,128)(2,1)}, u32[]{:S(2)}, u32[]{:S(2)}) collective-permute-start(bf16[256,1536]{1,0:T(8,128)(2,1)} %pad_maximum_fusion.5), channel_id=1, source_target_pairs={{0,2},{1,3},{2,4},{3,5},{4,6},{5,7},{6,8},{7,9},{8,10},{9,11},{10,... | collective-permute-start | bytes 2359304 | tf_op jit(solution)/shard_map/ppermute | solution.py:22
  202.4 2.9 copy-start.12
  205.5 3.2 copy-start.13
  205.8 3.3 copy-start.11
  209.1 15.6 %copy-start.17 = (f32[4,128,512]{2,1,0:T(8,128)}, f32[4,128,512]{2,1,0:T(8,128)S(1)}, u32[]{:S(2)}) copy-start(f32[4,128,512]{2,1,0:T(8,128)S(1)} %fusion.18) | copy-start | bytes 3145732
  229.5 3.8 copy-start.21
  229.9 12.2 %copy-start.14 = (f32[4,128,512]{2,1,0:T(8,128)}, f32[4,128,512]{2,1,0:T(8,128)S(1)}, u32[]{:S(2)}) copy-start(f32[4,128,512]{2,1,0:T(8,128)S(1)} %fusion.41) | copy-start | bytes 3145732
  242.1 5.3 %copy-start.16 = (bf16[128,512]{0,1:T(8,128)(2,1)S(1)}, bf16[128,512]{0,1:T(8,128)(2,1)}, u32[]{:S(2)}) copy-start(bf16[128,512]{0,1:T(8,128)(2,1)} %copy-done.15) | copy-start | bytes 393220
  252.9 3.9 %copy-start.2 = (f32[512,1536]{1,0:T(8,128)}, f32[512,1536]{1,0:T(8,128)S(1)}, u32[]{:S(2)}) copy-start(f32[512,1536]{1,0:T(8,128)S(1)} %pad_maximum_fusion) | copy-start | bytes 9437188
  252.9 2.9 copy-start.18
  252.9 3.1 copy-start.19
  252.9 3.5 copy-start.20
  254.2 108.1 %collective-permute-start.4 = (f32[256,1536]{1,0:T(8,128)}, f32[256,1536]{1,0:T(8,128)}, u32[]{:S(2)}, u32[]{:S(2)}) collective-permute-start(f32[256,1536]{1,0:T(8,128)} %slice.74), channel_id=1, source_target_pairs={{2,0},{3,1},{4,2},{5,3},{6,4},{7,5},{8,6},{9,7},{10,8},{11,9},{12,... | collective-permute-start | bytes 4718600 | tf_op jit(solution)/shard_map/ppermute | solution.py:22
  258.1 13.4 %copy-start.23 = (f32[128,12]{0,1:T(8,128)S(1)}, f32[128,12]{0,1:T(8,128)}, u32[]{:S(2)}) copy-start(f32[128,12]{0,1:T(8,128)} %copy-done.22) | copy-start | bytes 18436
  258.1 13.4 %copy-start.27 = (f32[128]{0:T(128)S(1)}, f32[128]{0:T(128)}, u32[]{:S(2)}) copy-start(f32[128]{0:T(128)} %param.15) | copy-start | bytes 1540
  258.1 105.9 %collective-permute-start.6 = (f32[256,1536]{0,1:T(8,128)}, f32[256,1536]{0,1:T(8,128)}, u32[]{:S(2)}, u32[]{:S(2)}) collective-permute-start(f32[256,1536]{0,1:T(8,128)} %slice.76), channel_id=1, source_target_pairs={{2,0},{3,1},{4,2},{5,3},{6,4},{7,5},{8,6},{9,7},{10,8},{11,9},{12,... | collective-permute-start | bytes 4718600 | tf_op jit(solution)/shard_map/ppermute | solution.py:22
  356.3 6.0 %copy-start.3 = (f32[512,1536]{1,0:T(8,128)S(1)}, f32[512,1536]{1,0:T(8,128)}, u32[]{:S(2)}) copy-start(f32[512,1536]{1,0:T(8,128)} %copy-done.2) | copy-start | bytes 9437188
  364.0 3.3 collective-permute-start.5
  365.8 1.5 copy-start.9
  365.8 1.9 copy-start.5
  365.8 1.9 copy-start.26
  366.8 7.1 %collective-permute-start.7 = (f32[128,1536]{0,1:T(8,128)}, f32[128,1536]{0,1:T(8,128)}, u32[]{:S(2)}, u32[]{:S(2)}) collective-permute-start(f32[128,1536]{0,1:T(8,128)} %constant_dynamic-slice_fusion), channel_id=1, source_target_pairs={{0,1},{1,0},{2,3},{3,2},{4,5},{5,4},{6,7},{7,6},{8,9},{9,8},{10,11... | collective-permute-start | bytes 2359304 | tf_op jit(solution)/shard_map/ppermute | solution.py:16
  367.4 1.8 copy-start.8
  367.4 1.8 copy-start.24
  367.9 6.0 %slice-start = ((s8[4718592]{0:T(1024)(128)(4,1)}), s8[524288]{0:T(1024)(128)(4,1)S(1)}, s32[]{:S(2)}) async-start(s8[4718592]{0:T(1024)(128)(4,1)} %bitcast.115), calls=%async_computation.3 | async-start | bytes 1048576
  369.1 4.8 %slice-start.1 = ((s8[4718592]{0:T(1024)(128)(4,1)}), s8[4194304]{0:T(1024)(128)(4,1)S(1)}, s32[]{:S(2)}) async-start(s8[4718592]{0:T(1024)(128)(4,1)} %bitcast.115), calls=%async_computation.4 | async-start | bytes 8388608
  369.1 4.8 %copy-start.10 = (f32[256,1536]{0,1:T(8,128)S(1)}, f32[256,1536]{0,1:T(8,128)}, u32[]{:S(2)}) copy-start(f32[256,1536]{0,1:T(8,128)} %copy-done.9) | copy-start | bytes 4718596
  369.2 8.4 %copy-start.1 = (bf16[128,1536]{1,0:T(8,128)(2,1)S(1)}, bf16[128,1536]{1,0:T(8,128)(2,1)}, u32[]{:S(2)}) copy-start(bf16[128,1536]{1,0:T(8,128)(2,1)} %param.10) | copy-start | bytes 1179652
Sparse Core Ops, SparseCore 0:
  10.3 56.0 all-gather.3
  68.7 51.9 all-gather.5
  123.0 51.9 all-gather.7
where the time goes:
time: 387 us; the launch traced here: 385 us
  waiting for transfers between devices  162 us (42%)
  blocking collectives  76.1 us (20%)
  matrix products  67.1 us (17%)
  other arithmetic  25.7 us (7%)
  local copies, waits for them, and re-layouts  23.7 us (6%)
  between operations  18.8 us (5%)
  starting transfers between devices  12 us (3%)
    psum x1, blocking collectives, per_device(): loss_sum = lax.psum(loss_part, 'tm')  76.1 us
    all_gather x1, waiting for transfers between devices, per_device(): lax.all_gather(w_key, 'tm', axis=0, tiled=True)  50.4 us
    all_gather x1, waiting for transfers between devices, per_device(): lax.all_gather(w_query, 'tm', axis=0, tiled=True)  48 us
    all_gather x1, waiting for transfers between devices, per_device(): lax.all_gather(w_value, 'tm', axis=0, tiled=True)  44.8 us
    ppermute x4, waiting for transfers between devices, from_behind(): return lax.ppermute(block, axis, route)  16.5 us
    dot_general x3, matrix products, back_project(): lax.dot_general(grad, weight, (((1,), (1,)), ((), ())), preferred_element...  14.3 us
    ppermute x4, starting transfers between devices, from_behind(): return lax.ppermute(block, axis, route)  10.8 us
    dot_general x3, matrix products, group_pass(): jnp.einsum('hqk,khd->qhd', score_grad, key_heads, preferred_element_type=...  10.2 us
  transfers between devices with their start and end apart: 11, of which 5 were waited for; matrix products, arithmetic and copies ran while one was open for 20% of the time, Pallas kernels for 0%

commit v1 on v0

v1 whole, which is shorter than its diff:
```python
import functools
import math

import jax
import jax.numpy as jnp
from jax import lax
from jax.experimental import pallas as pl
from jax.experimental.pallas import tpu as pltpu
from jax.sharding import PartitionSpec as P

epsilon = 1e-06
loss_scale = 32.0
QUAD = 4
MESH = pl.DeviceIdType.MESH
ORDER = (1, 2, 0)


def gather_kernel(
    nz, tok, tgt, wq, wk, wv, tokb, tgtb, wbuf,
    inj_recv, inj_send, inj_local,
    up_recv, up_send, dn_recv, dn_send, x_recv, x_send,
    tok_recv, tok_send, tok_local, tgt_recv, tgt_send, tgt_local,
):
    g, t = lax.axis_index("groups"), lax.axis_index("tm")
    z, k = t // QUAD, t % QUAD
    y, c = k // 2, k % 2
    part = wbuf.shape[3]
    weights = (wq, wk, wv)
    has_up, has_dn = z + 1 < nz, z > 0
    ynbr = (g, t + 2 - 4 * y)
    cnbr = (g, t + 1 - 2 * c)
    xnbr = (g + 1 - 2 * (g % 2), t)
    half = g % 2

    barrier = pltpu.get_barrier_semaphore()

    def greet(device):
        pl.semaphore_signal(barrier, inc=1, device_id=device, device_id_type=MESH)

    for d in range(1, QUAD):
        greet((g, QUAD * z + (k + d) % QUAD))
    greet(xnbr)

    @pl.when(has_up)
    def _():
        for m in range(QUAD):
            greet((g, QUAD * (z + 1) + m))

    @pl.when(has_dn)
    def _():
        for m in range(QUAD):
            greet((g, QUAD * (z - 1) + m))

    sides = jnp.where(has_up, 1, 0) + jnp.where(has_dn, 1, 0)
    pl.semaphore_wait(barrier, QUAD + QUAD * sides)

    def remote(src, dst, send_sem, recv_sem, device):
        return pltpu.make_async_remote_copy(
            src_ref=src, dst_ref=dst, send_sem=send_sem, recv_sem=recv_sem,
            device_id=device, device_id_type=MESH,
        )

    def columns(ref, m):
        return ref.at[:, pl.ds(pl.multiple_of(m * part, 128), part)]

    def inject(w, d):
        m = (k + d) % QUAD
        return remote(
            columns(weights[w], m), wbuf.at[w, t], inj_send.at[w, d - 1], inj_recv.at[w, k],
            (g, QUAD * z + m),
        )

    def injected(w, d):
        m = (k + d) % QUAD
        slot = wbuf.at[w, QUAD * z + m]
        return remote(slot, slot, inj_send.at[w, d - 1], inj_recv.at[w, m], (g, QUAD * z + m))

    def inject_own(w):
        return pltpu.make_async_copy(columns(weights[w], k), wbuf.at[w, t], inj_local.at[w])

    def piece(w, q, h):
        return wbuf.at[w, pl.ds(QUAD * q + 2 * h, 2)]

    def go_up(w, q):
        return remote(
            piece(w, q, half), piece(w, q, half), up_send.at[w, q], up_recv.at[w, q], (g, t + QUAD)
        )

    def go_dn(w, q):
        return remote(
            piece(w, q, half), piece(w, q, half), dn_send.at[w, q], dn_recv.at[w, q], (g, t - QUAD)
        )

    def go_x(w, q):
        return remote(
            piece(w, q, half), piece(w, q, half), x_send.at[w, q], x_recv.at[w, q], xnbr
        )

    def from_x(w, q):
        return remote(
            piece(w, q, 1 - half), piece(w, q, 1 - half), x_send.at[w, q], x_recv.at[w, q], xnbr
        )

    own_slot = 2 * (1 + y) + c
    their_slot = 2 * (2 - y) + c
    halo_slot = 6 * (1 - y) + c
    their_halo = 6 * y + c
    has_halo = jnp.where(y == 1, z, nz - 1 - z) > 0
    has_their_halo = jnp.where(y == 0, z, nz - 1 - z) > 0
    give_halo = jnp.where(y == 0, z, nz - 1 - z) > 0
    halo_to = (g, jnp.where(y == 0, t - QUAD, t + QUAD))
    halo_to_slot = 6 * (1 - y) + c

    def send_tok(src, slot, i, device):
        return remote(src, tokb.at[slot], tok_send.at[i], tok_recv.at[slot], device)

    own_y = send_tok(tok, own_slot, 0, ynbr)
    own_c = send_tok(tok, own_slot, 1, cnbr)
    own_z = send_tok(tok, halo_to_slot, 2, halo_to)
    halo_y = send_tok(tokb.at[halo_slot], halo_slot, 3, ynbr)
    halo_c = send_tok(tokb.at[halo_slot], halo_slot, 4, cnbr)
    their_c = send_tok(tokb.at[their_slot], their_slot, 5, cnbr)
    their_halo_c = send_tok(tokb.at[their_halo], their_halo, 6, cnbr)
    tok_own = pltpu.make_async_copy(tok, tokb.at[own_slot], tok_local.at[0])

    def tok_wait(slot):
        send_tok(tokb.at[slot], slot, 0, cnbr).wait_recv()

    def tgt_quad(d):
        m = (k + d) % QUAD
        return remote(
            columns(tgt, m), tgtb.at[k], tgt_send.at[d - 1], tgt_recv.at[k], (g, QUAD * z + m)
        )

    def tgt_before(m):
        return remote(
            columns(tgt, m), tgtb.at[QUAD + c], tgt_send.at[3 + m], tgt_recv.at[QUAD + c],
            (g, QUAD * (z - 1) + m),
        )

    tgt_own = pltpu.make_async_copy(columns(tgt, k), tgtb.at[k], tgt_local.at[0])

    def tgt_wait(slot):
        remote(
            tgtb.at[slot], tgtb.at[slot], tgt_send.at[0], tgt_recv.at[slot], cnbr
        ).wait_recv()

    gives_target = jnp.where(y == 0, z, 0) > 0

    for w in ORDER:
        for d in (2, 3, 1):
            inject(w, d).start()
        inject_own(w).start()
        if w == ORDER[0]:

            @pl.when(give_halo)
            def _():
                own_z.start()

            own_y.start()
            own_c.start()
            tok_own.start()
    for d in range(1, QUAD):
        tgt_quad(d).start()
    tgt_own.start()

    @pl.when(gives_target)
    def _():
        for m in range(QUAD):
            tgt_before(m).start()

    for w in ORDER:
        for d in range(1, QUAD):
            injected(w, d).wait_recv()
        inject_own(w).wait()

        @pl.when(has_up)
        def _():
            go_up(w, z).start()

        @pl.when(has_dn)
        def _():
            go_dn(w, z).start()

    tok_wait(their_slot)
    their_c.start()

    @pl.when(has_halo)
    def _():
        tok_wait(halo_slot)
        halo_y.start()
        halo_c.start()

    for s in range(1, nz):
        for w in ORDER:

            @pl.when(z - s >= 0)
            def _():
                go_up(w, z - s).wait_recv()
                go_x(w, z - s).start()

                @pl.when(has_up)
                def _():
                    go_up(w, z - s).start()

            @pl.when(z + s < nz)
            def _():
                go_dn(w, z + s).wait_recv()
                go_x(w, z + s).start()

                @pl.when(has_dn)
                def _():
                    go_dn(w, z + s).start()

        if s == 1:

            @pl.when(has_their_halo)
            def _():
                tok_wait(their_halo)
                their_halo_c.start()

    other = 1 - 2 * c
    tok_wait(2 + c + other)
    tok_wait(4 + c + other)

    @pl.when(has_dn)
    def _():
        tok_wait(c + other)

    @pl.when(has_up)
    def _():
        tok_wait(6 + c + other)

    for d in range(1, QUAD):
        tgt_wait((k + d) % QUAD)

    @pl.when(has_up)
    def _():
        tgt_wait(QUAD)
        tgt_wait(QUAD + 1)

    for s in range(1, nz):
        for w in ORDER:

            @pl.when(z - s >= 0)
            def _():
                from_x(w, z - s).wait_recv()

            @pl.when(z + s < nz)
            def _():
                from_x(w, z + s).wait_recv()

    tok_own.wait()
    tgt_own.wait()
    own_y.wait_send()
    own_c.wait_send()
    their_c.wait_send()

    @pl.when(give_halo)
    def _():
        own_z.wait_send()

    @pl.when(has_halo)
    def _():
        halo_y.wait_send()
        halo_c.wait_send()

    @pl.when(has_their_halo)
    def _():
        their_halo_c.wait_send()

    for d in range(1, QUAD):
        tgt_quad(d).wait_send()

    @pl.when(gives_target)
    def _():
        for m in range(QUAD):
            tgt_before(m).wait_send()

    for w in ORDER:
        for d in range(1, QUAD):
            inject(w, d).wait_send()

        @pl.when(has_up)
        def _():
            go_up(w, z).wait_send()

        @pl.when(has_dn)
        def _():
            go_dn(w, z).wait_send()

        for s in range(1, nz):

            @pl.when(z - s >= 0)
            def _():
                go_x(w, z - s).wait_send()

                @pl.when(has_up)
                def _():
                    go_up(w, z - s).wait_send()

            @pl.when(z + s < nz)
            def _():
                go_x(w, z + s).wait_send()

                @pl.when(has_dn)
                def _():
                    go_dn(w, z + s).wait_send()


def gather(tokens, target, w_query, w_key, w_value, n):
    nz = n // QUAD
    rows, width = tokens.shape
    depth = w_query.shape[0]
    part = w_query.shape[1] // QUAD
    dma = pltpu.SemaphoreType.DMA
    any_spec = pl.BlockSpec(memory_space=pl.ANY)
    return pl.pallas_call(
        functools.partial(gather_kernel, nz),
        out_shape=(
            jax.ShapeDtypeStruct((8, rows, width), jnp.bfloat16),
            jax.ShapeDtypeStruct((6, rows, part), jnp.bfloat16),
            jax.ShapeDtypeStruct((3, n, depth, part), jnp.bfloat16),
        ),
        in_specs=[any_spec] * 5,
        out_specs=(any_spec,) * 3,
        scratch_shapes=[
            dma((3, QUAD)), dma((3, QUAD - 1)), dma((3,)),
            dma((3, nz)), dma((3, nz)), dma((3, nz)), dma((3, nz)), dma((3, nz)), dma((3, nz)),
            dma((8,)), dma((7,)), dma((1,)), dma((6,)), dma((7,)), dma((1,)),
        ],
        compiler_params=pltpu.CompilerParams(collective_id=0, has_side_effects=True),
    )(tokens, target, w_query, w_key, w_value)


def layer_kernel(
    heads, head_size, block,
    info, weight, tok, tgt, w, qg, kg, out, loss,
    raw_q, raw_k, qn, kn, vn, dq, dk, dv, back,
):
    scale = 1.0 / math.sqrt(head_size)
    q_gain, k_gain = qg[...], kg[...]
    f32, bf16 = jnp.float32, jnp.bfloat16

    def normed(raw, gain):
        factor = lax.rsqrt(jnp.mean(raw * raw, axis=-1, keepdims=True) + epsilon)
        return (raw * factor * gain).astype(bf16)

    for b in range(4):
        rows = slice(b * block, (b + 1) * block)
        x = tok[rows, :]
        if b == 0:
            x = jnp.where(info[7] > 0, x, jnp.zeros_like(x))
        if b == 3:
            x = jnp.where(info[8] > 0, x, jnp.zeros_like(x))
        keys = jnp.dot(x, w[1], preferred_element_type=f32)
        values = jnp.dot(x, w[2], preferred_element_type=f32)
        if b > 0:
            queries = jnp.dot(x, w[0], preferred_element_type=f32)
        for h in range(heads):
            cols = slice(h * head_size, (h + 1) * head_size)
            kn[h, rows, :] = normed(keys[:, cols], k_gain)
            vn[h, rows, :] = values[:, cols].astype(bf16)
            if b > 0:
                qn[h, (b - 1) * block : b * block, :] = normed(queries[:, cols], q_gain)
            if b == 1 or b == 2:
                own = slice((b - 1) * block, b * block)
                raw_k[h, own, :] = keys[:, cols]
                raw_q[h, own, :] = queries[:, cols]

    dk[...] = jnp.zeros_like(dk)
    dv[...] = jnp.zeros_like(dv)
    loss[...] = jnp.zeros_like(loss)

    key_place = lax.broadcasted_iota(jnp.int32, (1, 2 * block), 1)
    in_own = key_place >= block
    key_pos = jnp.where(in_own, key_place - block, key_place)
    query_pos = lax.broadcasted_iota(jnp.int32, (block, 1), 0)
    dims_nt = (((1,), (1,)), ((), ()))
    dims_tn = (((0,), (0,)), ((), ()))

    for i in range(3):
        before = jnp.where(info[4 + i] > 0, info[i], 0)
        limit = jnp.where(in_own, info[i + 1], before)
        allowed = key_pos < limit
        row_weight = jnp.where(query_pos < info[i + 1], weight[i], 0.0)
        rows = slice(i * block, (i + 1) * block)
        span = slice(i * block, (i + 2) * block)
        for h in range(heads):
            cols = slice(h * head_size, (h + 1) * head_size)
            q = qn[h, rows, :]
            k = kn[h, span, :]
            v = vn[h, span, :]
            scores = lax.dot_general(q, k, dims_nt, preferred_element_type=f32) * scale
            expo = jnp.where(allowed, jnp.exp(scores), 0.0)
            probs = expo * (1.0 / jnp.sum(expo, axis=-1, keepdims=True))
            probs_cast = probs.astype(bf16)
            attended = jnp.dot(probs_cast, v, preferred_element_type=f32).astype(bf16)
            goal = tgt[rows, cols]
            if i == 2:
                goal = jnp.where(info[8] > 0, goal, jnp.zeros_like(goal))
            diff = attended.astype(f32) - goal.astype(f32)
            weighted = row_weight * diff
            if i < 2:
                squares = jnp.sum(weighted * diff, axis=0, keepdims=True)
                loss[0:1, :] += squares
            grad = (loss_scale * weighted).astype(bf16)
            prob_grad = lax.dot_general(grad, v, dims_nt, preferred_element_type=f32)
            delta = jnp.sum(probs * prob_grad, axis=-1, keepdims=True)
            score_grad = (probs * (prob_grad - delta) * scale).astype(bf16)
            if i < 2:
                dq[h, rows, :] = jnp.dot(score_grad, k, preferred_element_type=f32)
            if i < 2:
                own = slice(i * block, (i + 1) * block)
                dv[h, own, :] += lax.dot_general(
                    probs_cast[:, block:], grad, dims_tn, preferred_element_type=f32)
                dk[h, own, :] += lax.dot_general(
                    score_grad[:, block:], q, dims_tn, preferred_element_type=f32)
            if i > 0:
                own = slice((i - 1) * block, i * block)
                dv[h, own, :] += lax.dot_general(
                    probs_cast[:, :block], grad, dims_tn, preferred_element_type=f32)
                dk[h, own, :] += lax.dot_general(
                    score_grad[:, :block], q, dims_tn, preferred_element_type=f32)

    def norm_back(upstream, raw, gain):
        factor = lax.rsqrt(jnp.mean(raw * raw, axis=-1, keepdims=True) + epsilon)
        unit = raw * factor
        s = upstream * gain
        return (factor * (s - unit * jnp.mean(s * unit, axis=-1, keepdims=True))).astype(bf16)

    for h in range(heads):
        cols = slice(h * head_size, (h + 1) * head_size)
        back[0, :, cols] = norm_back(dq[h], raw_q[h], q_gain)
        back[1, :, cols] = norm_back(dk[h], raw_k[h], k_gain)
        back[2, :, cols] = dv[h].astype(bf16)

    depth = w.shape[1]
    step = 512
    for start in range(0, depth, step):
        total = lax.dot_general(
            back[0], w[0, start : start + step, :], dims_nt, preferred_element_type=f32)
        for j in (1, 2):
            total += lax.dot_general(
                back[j], w[j, start : start + step, :], dims_nt, preferred_element_type=f32)
        out[:, start : start + step] = total.astype(bf16)


def layer(info, weight, tok, tgt, w, q_gain, k_gain, block):
    head_size = q_gain.shape[0]
    depth, part = w.shape[1], w.shape[2]
    heads = part // head_size
    vmem = pl.BlockSpec(memory_space=pltpu.VMEM)
    smem = pl.BlockSpec(memory_space=pltpu.SMEM)
    f32, bf16 = jnp.float32, jnp.bfloat16
    return pl.pallas_call(
        functools.partial(layer_kernel, heads, head_size, block),
        out_shape=(
            jax.ShapeDtypeStruct((2 * block, depth), bf16),
            jax.ShapeDtypeStruct((8, 128), f32),
        ),
        in_specs=[smem, smem, vmem, vmem, vmem, vmem, vmem],
        out_specs=(vmem, vmem),
        scratch_shapes=[
            pltpu.VMEM((heads, 2 * block, head_size), f32),
            pltpu.VMEM((heads, 2 * block, head_size), f32),
            pltpu.VMEM((heads, 3 * block, head_size), bf16),
            pltpu.VMEM((heads, 4 * block, head_size), bf16),
            pltpu.VMEM((heads, 4 * block, head_size), bf16),
            pltpu.VMEM((heads, 2 * block, head_size), f32),
            pltpu.VMEM((heads, 2 * block, head_size), f32),
            pltpu.VMEM((heads, 2 * block, head_size), f32),
            pltpu.VMEM((3, 2 * block, part), bf16),
        ],
        compiler_params=pltpu.CompilerParams(vmem_limit_bytes=48 * 1024 * 1024),
    )(info, weight, tok, tgt, w, q_gain.reshape(1, head_size), k_gain.reshape(1, head_size))


def share_kernel(
    n, part, loss, out, loss_out, cbuf, ysend, yrecv, lbuf,
    c_send, c_recv, y_sem, l_send, l_recv,
):
    g, t = lax.axis_index("groups"), lax.axis_index("tm")
    k = t % QUAD
    y, c = k // 2, k % 2
    ynbr = (g, t + 2 - 4 * y)
    cnbr = (g, t + 1 - 2 * c)
    barrier = pltpu.get_barrier_semaphore()

    @pl.loop(1, n)
    def _(d):
        pl.semaphore_signal(
            barrier, inc=1, device_id=(g, (t + d) % n), device_id_type=MESH)

    pl.semaphore_wait(barrier, n - 1)

    def to_core(row):
        return pltpu.make_async_remote_copy(
            src_ref=part.at[2 * row + 1 - c], dst_ref=cbuf.at[row],
            send_sem=c_send.at[row], recv_sem=c_recv.at[row],
            device_id=cnbr, device_id_type=MESH,
        )

    to_core(1 - y).start()
    to_core(y).start()
    lbuf[t] = loss[...]

    def to_all(d):
        return pltpu.make_async_remote_copy(
            src_ref=loss, dst_ref=lbuf.at[t], send_sem=l_send.at[d],
            recv_sem=l_recv.at[t], device_id=(g, (t + d) % n), device_id_type=MESH,
        )

    def from_all(d):
        source = (t + d) % n
        return pltpu.make_async_remote_copy(
            src_ref=loss, dst_ref=lbuf.at[source], send_sem=l_send.at[d],
            recv_sem=l_recv.at[source], device_id=(g, source), device_id_type=MESH,
        )

    @pl.loop(1, n)
    def _(d):
        to_all(d).start()

    to_y = pltpu.make_async_remote_copy(
        src_ref=ysend, dst_ref=yrecv, send_sem=y_sem.at[0], recv_sem=y_sem.at[1],
        device_id=ynbr, device_id_type=MESH,
    )

    def arrived(row):
        return pltpu.make_async_remote_copy(
            src_ref=part.at[2 * row + 1 - c], dst_ref=cbuf.at[row],
            send_sem=c_send.at[row], recv_sem=c_recv.at[row],
            device_id=cnbr, device_id_type=MESH,
        )

    arrived(1 - y).wait_recv()
    ysend[...] = (
        part[2 * (1 - y) + c].astype(jnp.float32) + cbuf[1 - y].astype(jnp.float32)
    ).astype(jnp.bfloat16)
    to_y.start()
    arrived(y).wait_recv()

    @pl.loop(1, n)
    def _(d):
        from_all(d).wait_recv()

    total = jnp.sum(lbuf[...], axis=0)
    loss_out[...] = jnp.broadcast_to(jnp.sum(total), loss_out.shape)

    to_y.wait_recv()
    out[...] = (
        part[k].astype(jnp.float32) + cbuf[y].astype(jnp.float32) + yrecv[...].astype(jnp.float32)
    ).astype(jnp.bfloat16)
    to_y.wait_send()
    to_core(1 - y).wait_send()
    to_core(y).wait_send()

    @pl.loop(1, n)
    def _(d):
        to_all(d).wait_send()


def share(part, loss, n):
    _, rows, depth = part.shape
    dma = pltpu.SemaphoreType.DMA
    vmem = pl.BlockSpec(memory_space=pltpu.VMEM)
    bf16 = jnp.bfloat16
    return pl.pallas_call(
        functools.partial(share_kernel, n),
        out_shape=(
            jax.ShapeDtypeStruct((rows, depth), bf16),
            jax.ShapeDtypeStruct((8, 128), jnp.float32),
        ),
        in_specs=[vmem, vmem],
        out_specs=(vmem, vmem),
        scratch_shapes=[
            pltpu.VMEM((2, rows, depth), bf16),
            pltpu.VMEM((rows, depth), bf16),
            pltpu.VMEM((rows, depth), bf16),
            pltpu.VMEM((n, 8, 128), jnp.float32),
            dma((2,)), dma((2,)), dma((2,)), dma((n,)), dma((n,)),
        ],
        compiler_params=pltpu.CompilerParams(
            collective_id=1, has_side_effects=True, vmem_limit_bytes=24 * 1024 * 1024),
    )(part, loss)


def per_device(
    tokens, target, w_query, w_key, w_value, q_gain, k_gain, block_weight, block_reset, valid_count
):
    rows, width = tokens.shape
    n = lax.axis_size("tm")
    nz = n // QUAD
    block = 2 * rows
    z = lax.axis_index("tm") // QUAD
    blocks = valid_count.shape[0]
    index = 2 * z - 1 + jnp.arange(4, dtype=jnp.int32)
    inside = (index >= 0) & (index < blocks)
    hit = index[:, None] == jnp.arange(blocks, dtype=jnp.int32)[None, :]
    count = jnp.sum(jnp.where(hit, valid_count[None, :], 0), axis=1)
    reset = jnp.sum(jnp.where(hit, block_reset[None, :], 0), axis=1)
    weight = jnp.sum(jnp.where(hit, block_weight[None, :], 0.0), axis=1)[1:]
    count = jnp.where(inside | (index < 0), count, 1)
    sees = ((index[1:] > 0) & (reset[1:] == 0)).astype(jnp.int32)
    flags = jnp.stack([z > 0, z < nz - 1]).astype(jnp.int32)
    info = jnp.concatenate([count, sees, flags])

    tok, tgt, w = gather(tokens, target, w_query, w_key, w_value, n)
    part, loss = layer(
        info,
        weight,
        tok.reshape(8 * rows, width),
        tgt.reshape(6 * rows, -1),
        w.reshape(3, width, -1),
        q_gain,
        k_gain,
        block,
    )
    grad, loss_sum = share(part.reshape(QUAD, rows, width), loss, n)
    size = rows * n * w_query.shape[1]
    return grad, (loss_sum[0, :1] / size).reshape(1)


def solution(mesh):
    return jax.shard_map(
        per_device,
        mesh=mesh,
        in_specs=(
            P(("groups", "tm"), None),
            P(("groups", "tm"), None),
            P("tm", None),
            P("tm", None),
            P("tm", None),
            P(),
            P(),
            P("groups"),
            P("groups"),
            P("groups"),
        ),
        out_specs=(P(("groups", "tm"), None), P("groups")),
        check_vma=False,
    )
```

time: 387 us -> 105 us (0.27)
  waiting for transfers between devices: 162 us -> 0 us
  Pallas kernels: 0 us -> 94.2 us
  blocking collectives: 76.1 us -> 0 us
  matrix products: 67.1 us -> 0 us
  other arithmetic: 25.7 us -> 1.96 us
  local copies, waits for them, and re-layouts: 23.7 us -> 5.59 us
  between operations: 18.8 us -> 2.48 us
  starting transfers between devices: 12 us -> 0 us
    all_gather x3 -> x0, waiting for transfers between devices: 143 us -> none  [the longest x1 50.4 us: per_device(): lax.all_gather(w_key, 'tm', axis=0, tiled=True)]
    pallas_call x0 -> x3, Pallas kernels: none -> 94.2 us  [the longest x1 58.9 us: gather(): pl.pallas_call(functools.partial(gather_kernel, nz), out_shape=(jax.Shape...]
    psum x1 -> x0, blocking collectives: 76.1 us -> none  [per_device(): loss_sum = lax.psum(loss_part, 'tm')]
    dot_general x24 -> x0, matrix products: 62.6 us -> none  [the longest x3 14.3 us: back_project(): lax.dot_general(grad, weight, (((1,), (1,)), ((), ())), preferred_element...]
    ppermute x8 -> x0, waiting for transfers between devices: 16.5 us -> none  [the longest x4 16.5 us: from_behind(): return lax.ppermute(block, axis, route)]
    ppermute x8 -> x0, starting transfers between devices: 11.9 us -> none  [the longest x4 10.8 us: from_behind(): return lax.ppermute(block, axis, route)]
    mul x10 -> x0, local copies, waits for them, and re-layouts: 10.1 us -> none  [the longest x4 4.49 us: norm_backward(): unit * jnp.mean(shaped * unit, axis=-1, keepdims=True)]
    concatenate x7 -> x1, other arithmetic: 7.55 us -> 0.08 us  [per_device(): info = jnp.concatenate([count, sees, flags])]
  transfers between devices with their start and end apart: 11 -> 0, of which waited for: 5 -> 0; matrix products, arithmetic and copies ran while one was open for 20% -> 0% of each run, Pallas kernels for 0% -> 0%
where the time goes in v1:
time: 105 us; the launch traced here: 104 us
  Pallas kernels  94.2 us (90%)
  local copies, waits for them, and re-layouts  5.59 us (5%)
  between operations  2.48 us (2%)
  other arithmetic  1.96 us (2%)
    pallas_call x1, Pallas kernels, gather(): pl.pallas_call(functools.partial(gather_kernel, nz), out_shape=(jax.Shape...  58.9 us
    pallas_call x1, Pallas kernels, share(): pl.pallas_call(functools.partial(share_kernel, n), out_shape=(jax.ShapeDt...  18.1 us
    pallas_call x1, Pallas kernels, layer(): pl.pallas_call(functools.partial(layer_kernel, heads, head_size, block),...  17.2 us
    unnamed x9, local copies, waits for them, and re-layouts  5 us

profile of v1, /device:TPU:0, one launch (start us, length us, event | category | flops | bytes accessed | tf_op | source)
XLA Modules:
  0.0 104.3 jit_solution(4184715875394707690)
XLA Ops:
  0.6 0.1 add_convert_fusion
  0.7 0.8 select_reduce_fusion
  1.6 0.1 slice.14.weight
  1.6 0.9 select_reduce_fusion.2
  2.5 0.1 and_convert_fusion
  2.6 0.1 pad_add_fusion.info
  2.7 58.9 %shard_map.113 = (bf16[8,128,1536]{2,1,0:T(8,128)(2,1)}, bf16[6,128,384]{2,1,0:T(8,128)(2,1)}, bf16[3,16,96,384]{3,2,1,0:T(8,128)(2,1)}) custom-call(bf16[128,1536]{1,0:T(8,128)(2,1)} %tok.1, bf16[128,1536]{1,0:T(8,128)(2,1)} %tgt.1, bf16[96,1536]{1,0:T(8,128)(2,1)} %wq.1, bf16[96,1536]{1,0:T(8,128)(2,1)} %wk.1, bf16[96,1536]{1,0:T(8,128)(2,1)} %wv.1), custom_call_target="tpu_custom_call" | custom-call | tf_op jit(solution)/shard_map/pallas_call | solution.py:318
  61.6 0.0 copy-start
  61.6 1.9 %copy-done = bf16[8,128,1536]{2,1,0:T(8,128)(2,1)S(1)} copy-done((bf16[8,128,1536]{2,1,0:T(8,128)(2,1)S(1)}, bf16[8,128,1536]{2,1,0:T(8,128)(2,1)}, u32[]{:S(2)}) %copy-start) | copy-done | bytes 3145752
  63.5 0.0 copy-start.1
  63.5 1.1 %copy-done.1 = bf16[6,128,384]{2,1,0:T(8,128)(2,1)S(1)} copy-done((bf16[6,128,384]{2,1,0:T(8,128)(2,1)S(1)}, bf16[6,128,384]{2,1,0:T(8,128)(2,1)}, u32[]{:S(2)}) %copy-start.1) | copy-done | bytes 589848
  64.6 0.0 copy-start.2
  64.6 0.7 copy-done.2
  65.2 0.0 copy-start.3
  65.2 0.7 copy-done.3
  65.9 17.2 %shard_map.114 = (bf16[512,1536]{1,0:T(8,128)(2,1)S(1)}, f32[8,128]{1,0:T(8,128)S(1)}) custom-call(s32[9]{0:T(128)S(1)} %pad_add_fusion.info, f32[3]{0:T(128)S(1)} %slice.14.weight, bf16[1024,1536]{1,0:T(8,128)(2,1)S(1)} %bitcast.9, bf16[768,384]{1,0:T(8,128)(2,1)S(1)} %bitcast.11, bf16[3,1536,384]{2,1,0:T(8,128)(2,1)} %bitcast.14, f32[1,128]{1,0:T(1,128)S(1)} %bitcast.12, ...), custom_call_target="tpu_custom_call" | custom-call | tf_op jit(solution)/shard_map/pallas_call | solution.py:456
  83.1 18.1 %shard_map.115 = (bf16[128,1536]{1,0:T(8,128)(2,1)S(1)}, f32[8,128]{1,0:T(8,128)S(1)}) custom-call(bf16[4,128,1536]{2,1,0:T(8,128)(2,1)S(1)} %bitcast.10, f32[8,128]{1,0:T(8,128)S(1)} %get-tuple-element.13.loss), custom_call_target="tpu_custom_call" | custom-call | tf_op jit(solution)/shard_map/pallas_call | solution.py:569
  101.2 0.5 slice.15
  102.4 0.7 copy.13
  (2 shorter events, 0.0 us)
Async XLA Ops:
  61.6 1.9 %copy-start = (bf16[8,128,1536]{2,1,0:T(8,128)(2,1)S(1)}, bf16[8,128,1536]{2,1,0:T(8,128)(2,1)}, u32[]{:S(2)}) copy-start(bf16[8,128,1536]{2,1,0:T(8,128)(2,1)} %get-tuple-element.9) | copy-start | bytes 9437188
  63.5 1.1 %copy-start.1 = (bf16[6,128,384]{2,1,0:T(8,128)(2,1)S(1)}, bf16[6,128,384]{2,1,0:T(8,128)(2,1)}, u32[]{:S(2)}) copy-start(bf16[6,128,384]{2,1,0:T(8,128)(2,1)} %get-tuple-element.10) | copy-start | bytes 1769476
  64.6 0.7 copy-start.2
  65.2 0.7 copy-start.3

commit v2 on v1

--- a/solution.py
+++ b/solution.py
@@ -157,17 +157,9 @@
             def _():
                 own_z.start()
 
-            own_y.start()
-            own_c.start()
-            tok_own.start()
-    for d in range(1, QUAD):
-        tgt_quad(d).start()
+    own_c.start()
+    tok_own.start()
     tgt_own.start()
-
-    @pl.when(gives_target)
-    def _():
-        for m in range(QUAD):
-            tgt_before(m).start()
 
     for w in ORDER:
         for d in range(1, QUAD):
@@ -182,42 +174,60 @@
         def _():
             go_dn(w, z).start()
 
-    tok_wait(their_slot)
-    their_c.start()
-
-    @pl.when(has_halo)
-    def _():
-        tok_wait(halo_slot)
-        halo_y.start()
-        halo_c.start()
-
+    own_y.start()
+    for d in range(1, QUAD):
+        tgt_quad(d).start()
+
+    @pl.when(gives_target)
+    def _():
+        for m in range(QUAD):
+            tgt_before(m).start()
+
+    def relay_halo():
+        @pl.when(has_halo)
+        def _():
+            tok_wait(halo_slot)
+            halo_y.start()
+            halo_c.start()
+
+    def relay_theirs():
+        tok_wait(their_slot)
+        their_c.start()
+
+    def relay_their_halo():
+        @pl.when(has_their_halo)
+        def _():
+            tok_wait(their_halo)
+            their_halo_c.start()
+
+    tasks = [relay_halo, relay_theirs, relay_their_halo]
     for s in range(1, nz):
         for w in ORDER:
 
             @pl.when(z - s >= 0)
             def _():
                 go_up(w, z - s).wait_recv()
-                go_x(w, z - s).start()
 
                 @pl.when(has_up)
                 def _():
                     go_up(w, z - s).start()
 
+                go_x(w, z - s).start()
+
             @pl.when(z + s < nz)
             def _():
                 go_dn(w, z + s).wait_recv()
-                go_x(w, z + s).start()
 
                 @pl.when(has_dn)
                 def _():
                     go_dn(w, z + s).start()
 
-        if s == 1:
-
-            @pl.when(has_their_halo)
-            def _():
-                tok_wait(their_halo)
-                their_halo_c.start()
+                go_x(w, z + s).start()
+
+        if tasks:
+            tasks.pop(0)()
+    for task in tasks:
+        task()
 
     other = 1 - 2 * c
     tok_wait(2 + c + other)
@@ -335,9 +345,37 @@
 
 def layer_kernel(
     heads, head_size, block,
-    info, weight, tok, tgt, w, qg, kg, out, loss,
-    raw_q, raw_k, qn, kn, vn, dq, dk, dv, back,
+    valid_count, block_reset, block_weight, tok_hbm, tgt_hbm, w_hbm, qg, kg, back, loss,
+    tok, tgt, w, raw_q, raw_k, qn, kn, vn, dq, dk, dv, sems,
 ):
+    w_copies = [pltpu.make_async_copy(w_hbm.at[j], w.at[j], sems.at[j]) for j in range(3)]
+    tok_copies = [
+        pltpu.make_async_copy(
+            tok_hbm.at[b * block : (b + 1) * block], tok.at[b * block : (b + 1) * block],
+            sems.at[3 + b])
+        for b in range(4)
+    ]
+    tgt_copy = pltpu.make_async_copy(tgt_hbm, tgt, sems.at[7])
+    w_copies[1].start()
+    tok_copies[0].start()
+    w_copies[2].start()
+    w_copies[0].start()
+    for b in range(1, 4):
+        tok_copies[b].start()
+    tgt_copy.start()
+
+    z = lax.axis_index("tm") // QUAD
+    blocks = valid_count.shape[0]
+    has_before = z > 0
+    has_after = 2 * z + 2 < blocks
+    places = [jnp.maximum(2 * z - 1, 0), 2 * z, 2 * z + 1, jnp.minimum(2 * z + 2, blocks - 1)]
+    counts = [valid_count[p] for p in places]
+    counts[0] = jnp.where(has_before, counts[0], 0)
+    sees = [block_reset[p] == 0 for p in places[1:]]
+    sees[0] = sees[0] & has_before
+    weights = [block_weight[p] for p in places[1:]]
+    weights[2] = jnp.where(has_after, weights[2], 0.0)
+
     scale = 1.0 / math.sqrt(head_size)
     q_gain, k_gain = qg[...], kg[...]
     f32, bf16 = jnp.float32, jnp.bfloat16
@@ -348,13 +386,19 @@
 
     for b in range(4):
         rows = slice(b * block, (b + 1) * block)
+        tok_copies[b].wait()
         x = tok[rows, :]
         if b == 0:
-            x = jnp.where(info[7] > 0, x, jnp.zeros_like(x))
+            x = jnp.where(has_before, x, jnp.zeros_like(x))
+            w_copies[1].wait()
         if b == 3:
-            x = jnp.where(info[8] > 0, x, jnp.zeros_like(x))
+            x = jnp.where(has_after, x, jnp.zeros_like(x))
         keys = jnp.dot(x, w[1], preferred_element_type=f32)
+        if b == 0:
+            w_copies[2].wait()
         values = jnp.dot(x, w[2], preferred_element_type=f32)
+        if b == 1:
+            w_copies[0].wait()
         if b > 0:
             queries = jnp.dot(x, w[0], preferred_element_type=f32)
         for h in range(heads):
@@ -368,6 +412,7 @@
                 raw_k[h, own, :] = keys[:, cols]
                 raw_q[h, own, :] = queries[:, cols]
 
+    tgt_copy.wait()
     dk[...] = jnp.zeros_like(dk)
     dv[...] = jnp.zeros_like(dv)
     loss[...] = jnp.zeros_like(loss)
@@ -380,10 +425,10 @@
     dims_tn = (((0,), (0,)), ((), ()))
 
     for i in range(3):
-        before = jnp.where(info[4 + i] > 0, info[i], 0)
-        limit = jnp.where(in_own, info[i + 1], before)
+        before = jnp.where(sees[i], counts[i], 0)
+        limit = jnp.where(in_own, counts[i + 1], before)
         allowed = key_pos < limit
-        row_weight = jnp.where(query_pos < info[i + 1], weight[i], 0.0)
+        row_weight = jnp.where(query_pos < counts[i + 1], weights[i], 0.0)
         rows = slice(i * block, (i + 1) * block)
         span = slice(i * block, (i + 2) * block)
         for h in range(heads):
@@ -398,7 +443,7 @@
             attended = jnp.dot(probs_cast, v, preferred_element_type=f32).astype(bf16)
             goal = tgt[rows, cols]
             if i == 2:
-                goal = jnp.where(info[8] > 0, goal, jnp.zeros_like(goal))
+                goal = jnp.where(has_after, goal, jnp.zeros_like(goal))
             diff = attended.astype(f32) - goal.astype(f32)
             weighted = row_weight * diff
             if i < 2:
@@ -435,33 +480,27 @@
         back[1, :, cols] = norm_back(dk[h], raw_k[h], k_gain)
         back[2, :, cols] = dv[h].astype(bf16)
 
-    depth = w.shape[1]
-    step = 512
-    for start in range(0, depth, step):
-        total = lax.dot_general(
-            back[0], w[0, start : start + step, :], dims_nt, preferred_element_type=f32)
-        for j in (1, 2):
-            total += lax.dot_general(
-                back[j], w[j, start : start + step, :], dims_nt, preferred_element_type=f32)
-        out[:, start : start + step] = total.astype(bf16)
-
-
-def layer(info, weight, tok, tgt, w, q_gain, k_gain, block):
+
+def layer(valid_count, block_reset, block_weight, tok, tgt, w, q_gain, k_gain, block):
     head_size = q_gain.shape[0]
     depth, part = w.shape[1], w.shape[2]
     heads = part // head_size
     vmem = pl.BlockSpec(memory_space=pltpu.VMEM)
     smem = pl.BlockSpec(memory_space=pltpu.SMEM)
+    any_spec = pl.BlockSpec(memory_space=pl.ANY)
     f32, bf16 = jnp.float32, jnp.bfloat16
     return pl.pallas_call(
         functools.partial(layer_kernel, heads, head_size, block),
         out_shape=(
-            jax.ShapeDtypeStruct((2 * block, depth), bf16),
+            jax.ShapeDtypeStruct((3, 2 * block, part), bf16),
             jax.ShapeDtypeStruct((8, 128), f32),
         ),
-        in_specs=[smem, smem, vmem, vmem, vmem, vmem, vmem],
+        in_specs=[smem, smem, smem, any_spec, any_spec, any_spec, vmem, vmem],
         out_specs=(vmem, vmem),
         scratch_shapes=[
+            pltpu.VMEM(tok.shape, bf16),
+            pltpu.VMEM(tgt.shape, bf16),
+            pltpu.VMEM(w.shape, bf16),
             pltpu.VMEM((heads, 2 * block, head_size), f32),
             pltpu.VMEM((heads, 2 * block, head_size), f32),
             pltpu.VMEM((heads, 3 * block, head_size), bf16),
@@ -470,21 +509,38 @@
             pltpu.VMEM((heads, 2 * block, head_size), f32),
             pltpu.VMEM((heads, 2 * block, head_size), f32),
             pltpu.VMEM((heads, 2 * block, head_size), f32),
-            pltpu.VMEM((3, 2 * block, part), bf16),
+            pltpu.SemaphoreType.DMA((8,)),
         ],
-        compiler_params=pltpu.CompilerParams(vmem_limit_bytes=48 * 1024 * 1024),
-    )(info, weight, tok, tgt, w, q_gain.reshape(1, head_size), k_gain.reshape(1, head_size))
+        compiler_params=pltpu.CompilerParams(vmem_limit_bytes=56 * 1024 * 1024),
+    )(
+        valid_count, block_reset, block_weight, tok, tgt, w,
+        q_gain.reshape(1, head_size), k_gain.reshape(1, head_size),
+    )
+
+
+CHUNKS = 3
 
 
 def share_kernel(
-    n, part, loss, out, loss_out, cbuf, ysend, yrecv, lbuf,
-    c_send, c_recv, y_sem, l_send, l_recv,
+    n, back, w_hbm, loss, out, loss_out, w, part, cbuf, ysend, yrecv, lbuf,
+    w_sem, c_send, c_recv, y_send, y_recv, l_send, l_recv,
 ):
     g, t = lax.axis_index("groups"), lax.axis_index("tm")
     k = t % QUAD
     y, c = k // 2, k % 2
     ynbr = (g, t + 2 - 4 * y)
     cnbr = (g, t + 1 - 2 * c)
+    f32, bf16 = jnp.float32, jnp.bfloat16
+    rows, depth = out.shape
+    step = depth // CHUNKS
+
+    def w_copy(i):
+        span = slice(i * step, (i + 1) * step)
+        return pltpu.make_async_copy(w_hbm.at[:, span], w.at[:, span], w_sem.at[i])
+
+    for i in range(CHUNKS):
+        w_copy(i).start()
+
     barrier = pltpu.get_barrier_semaphore()
 
     @pl.loop(1, n)
@@ -492,18 +548,36 @@
         pl.semaphore_signal(
             barrier, inc=1, device_id=(g, (t + d) % n), device_id_type=MESH)
 
-    pl.semaphore_wait(barrier, n - 1)
-
-    def to_core(row):
+    def compute(i):
+        span = slice(i * step, (i + 1) * step)
+        w_copy(i).wait()
+        total = None
+        for j in range(3):
+            term = lax.dot_general(
+                back[j], w[j, span, :], (((1,), (1,)), ((), ())), preferred_element_type=f32)
+            total = term if total is None else total + term
+        for m in range(QUAD):
+            part[i, m] = total[m * rows : (m + 1) * rows].astype(bf16)
+
+    def to_core(i, row):
         return pltpu.make_async_remote_copy(
-            src_ref=part.at[2 * row + 1 - c], dst_ref=cbuf.at[row],
-            send_sem=c_send.at[row], recv_sem=c_recv.at[row],
+            src_ref=part.at[i, 2 * row + 1 - c], dst_ref=cbuf.at[i, row],
+            send_sem=c_send.at[i, row], recv_sem=c_recv.at[i, row],
             device_id=cnbr, device_id_type=MESH,
         )
 
-    to_core(1 - y).start()
-    to_core(y).start()
-    lbuf[t] = loss[...]
+    def to_y(i):
+        return pltpu.make_async_remote_copy(
+            src_ref=ysend.at[i], dst_ref=yrecv.at[i], send_sem=y_send.at[i],
+            recv_sem=y_recv.at[i], device_id=ynbr, device_id_type=MESH,
+        )
+
+    def pass_on(i):
+        to_core(i, 1 - y).wait_recv()
+        ysend[i] = (
+            part[i, 2 * (1 - y) + c].astype(f32) + cbuf[i, 1 - y].astype(f32)
+        ).astype(bf16)
+        to_y(i).start()
 
     def to_all(d):
         return pltpu.make_async_remote_copy(
@@ -518,29 +592,23 @@
             recv_sem=l_recv.at[source], device_id=(g, source), device_id_type=MESH,
         )
 
+    compute(0)
+    lbuf[t] = loss[...]
+    pl.semaphore_wait(barrier, n - 1)
+    to_core(0, 1 - y).start()
+    to_core(0, y).start()
+
+    for i in range(1, CHUNKS):
+        compute(i)
+        to_core(i, 1 - y).start()
+        to_core(i, y).start()
+        pass_on(i - 1)
+    pass_on(CHUNKS - 1)
+
     @pl.loop(1, n)
     def _(d):
         to_all(d).start()
 
-    to_y = pltpu.make_async_remote_copy(
-        src_ref=ysend, dst_ref=yrecv, send_sem=y_sem.at[0], recv_sem=y_sem.at[1],
-        device_id=ynbr, device_id_type=MESH,
-    )
-
-    def arrived(row):
-        return pltpu.make_async_remote_copy(
-            src_ref=part.at[2 * row + 1 - c], dst_ref=cbuf.at[row],
-            send_sem=c_send.at[row], recv_sem=c_recv.at[row],
-            device_id=cnbr, device_id_type=MESH,
-        )
-
-    arrived(1 - y).wait_recv()
-    ysend[...] = (
-        part[2 * (1 - y) + c].astype(jnp.float32) + cbuf[1 - y].astype(jnp.float32)
-    ).astype(jnp.bfloat16)
-    to_y.start()
-    arrived(y).wait_recv()
-
     @pl.loop(1, n)
     def _(d):
         from_all(d).wait_recv()
@@ -548,21 +616,26 @@
     total = jnp.sum(lbuf[...], axis=0)
     loss_out[...] = jnp.broadcast_to(jnp.sum(total), loss_out.shape)
 
-    to_y.wait_recv()
-    out[...] = (
-        part[k].astype(jnp.float32) + cbuf[y].astype(jnp.float32) + yrecv[...].astype(jnp.float32)
-    ).astype(jnp.bfloat16)
-    to_y.wait_send()
-    to_core(1 - y).wait_send()
-    to_core(y).wait_send()
+    for i in range(CHUNKS):
+        to_core(i, y).wait_recv()
+        to_y(i).wait_recv()
+        out[:, i * step : (i + 1) * step] = (
+            part[i, k].astype(f32) + cbuf[i, y].astype(f32) + yrecv[i].astype(f32)
+        ).astype(bf16)
+    for i in range(CHUNKS):
+        to_y(i).wait_send()
+        to_core(i, 1 - y).wait_send()
+        to_core(i, y).wait_send()
 
     @pl.loop(1, n)
     def _(d):
         to_all(d).wait_send()
 
 
-def share(part, loss, n):
-    _, rows, depth = part.shape
+def share(back, w, loss, n):
+    rows = back.shape[1] // QUAD
+    depth = w.shape[1]
+    step = depth // CHUNKS
     dma = pltpu.SemaphoreType.DMA
     vmem = pl.BlockSpec(memory_space=pltpu.VMEM)
     bf16 = jnp.bfloat16
@@ -572,18 +645,21 @@
             jax.ShapeDtypeStruct((rows, depth), bf16),
             jax.ShapeDtypeStruct((8, 128), jnp.float32),
         ),
-        in_specs=[vmem, vmem],
+        in_specs=[vmem, pl.BlockSpec(memory_space=pl.ANY), vmem],
         out_specs=(vmem, vmem),
         scratch_shapes=[
-            pltpu.VMEM((2, rows, depth), bf16),
-            pltpu.VMEM((rows, depth), bf16),
-            pltpu.VMEM((rows, depth), bf16),
+            pltpu.VMEM(w.shape, bf16),
+            pltpu.VMEM((CHUNKS, QUAD, rows, step), bf16),
+            pltpu.VMEM((CHUNKS, 2, rows, step), bf16),
+            pltpu.VMEM((CHUNKS, rows, step), bf16),
+            pltpu.VMEM((CHUNKS, rows, step), bf16),
             pltpu.VMEM((n, 8, 128), jnp.float32),
-            dma((2,)), dma((2,)), dma((2,)), dma((n,)), dma((n,)),
+            dma((CHUNKS,)), dma((CHUNKS, 2)), dma((CHUNKS, 2)), dma((CHUNKS,)), dma((CHUNKS,)),
+            dma((n,)), dma((n,)),
         ],
         compiler_params=pltpu.CompilerParams(
-            collective_id=1, has_side_effects=True, vmem_limit_bytes=24 * 1024 * 1024),
-    )(part, loss)
+            collective_id=1, has_side_effects=True, vmem_limit_bytes=48 * 1024 * 1024),
+    )(back, w, loss)
 
 
 def per_device(
@@ -591,33 +667,21 @@
 ):
     rows, width = tokens.shape
     n = lax.axis_size("tm")
-    nz = n // QUAD
     block = 2 * rows
-    z = lax.axis_index("tm") // QUAD
-    blocks = valid_count.shape[0]
-    index = 2 * z - 1 + jnp.arange(4, dtype=jnp.int32)
-    inside = (index >= 0) & (index < blocks)
-    hit = index[:, None] == jnp.arange(blocks, dtype=jnp.int32)[None, :]
-    count = jnp.sum(jnp.where(hit, valid_count[None, :], 0), axis=1)
-    reset = jnp.sum(jnp.where(hit, block_reset[None, :], 0), axis=1)
-    weight = jnp.sum(jnp.where(hit, block_weight[None, :], 0.0), axis=1)[1:]
-    count = jnp.where(inside | (index < 0), count, 1)
-    sees = ((index[1:] > 0) & (reset[1:] == 0)).astype(jnp.int32)
-    flags = jnp.stack([z > 0, z < nz - 1]).astype(jnp.int32)
-    info = jnp.concatenate([count, sees, flags])
-
     tok, tgt, w = gather(tokens, target, w_query, w_key, w_value, n)
-    part, loss = layer(
-        info,
-        weight,
+    w = w.reshape(3, width, -1)
+    back, loss = layer(
+        valid_count,
+        block_reset,
+        block_weight,
         tok.reshape(8 * rows, width),
         tgt.reshape(6 * rows, -1),
-        w.reshape(3, width, -1),
+        w,
         q_gain,
         k_gain,
         block,
     )
-    grad, loss_sum = share(part.reshape(QUAD, rows, width), loss, n)
+    grad, loss_sum = share(back, w, loss, n)
     size = rows * n * w_query.shape[1]
     return grad, (loss_sum[0, :1] / size).reshape(1)
 

time: 105 us -> 96.5 us (0.919)
  Pallas kernels: 94.2 us -> 90.6 us
  local copies, waits for them, and re-layouts: 5.59 us -> 3.22 us
  other arithmetic: 1.96 us -> 0 us
    pallas_call x1, Pallas kernels: 18.1 us -> 14.5 us  [share(): pl.pallas_call(functools.partial(share_kernel, n), out_shape=(jax.ShapeDt...]
    unnamed x9 -> x7, local copies, waits for them, and re-layouts: 5 us -> 2.7 us
    reduce_sum x2 -> x0, other arithmetic: 1.72 us -> none  [the longest x1 0.88 us: per_device(): count = jnp.sum(jnp.where(hit, valid_count[None, :], 0), axis=1)]
where the time goes in v2:
time: 96.5 us; the launch traced here: 96.3 us
  Pallas kernels  90.6 us (94%)
  local copies, waits for them, and re-layouts  3.22 us (3%)
  between operations  2.46 us (3%)
    pallas_call x1, Pallas kernels, gather(): pl.pallas_call(functools.partial(gather_kernel, nz), out_shape=(jax.Shape...  59 us
    pallas_call x1, Pallas kernels, layer(): pl.pallas_call(functools.partial(layer_kernel, heads, head_size, block),...  17.1 us
    pallas_call x1, Pallas kernels, share(): pl.pallas_call(functools.partial(share_kernel, n), out_shape=(jax.ShapeDt...  14.5 us
    unnamed x7, local copies, waits for them, and re-layouts  2.7 us

profile of v2, /device:TPU:0, one launch (start us, length us, event | category | flops | bytes accessed | tf_op | source)
XLA Modules:
  0.0 96.3 jit_solution(12200874822820229652)
XLA Ops:
  0.6 59.0 %shard_map.113 = (bf16[8,128,1536]{2,1,0:T(8,128)(2,1)}, bf16[6,128,384]{2,1,0:T(8,128)(2,1)}, bf16[3,16,96,384]{3,2,1,0:T(8,128)(2,1)}) custom-call(bf16[128,1536]{1,0:T(8,128)(2,1)} %tok.1, bf16[128,1536]{1,0:T(8,128)(2,1)} %tgt.1, bf16[96,1536]{1,0:T(8,128)(2,1)} %wq.1, bf16[96,1536]{1,0:T(8,128)(2,1)} %wk.1, bf16[96,1536]{1,0:T(8,128)(2,1)} %wv.1), custom_call_target="tpu_custom_call" | custom-call | tf_op jit(solution)/shard_map/pallas_call | solution.py:328
  59.6 0.0 copy-start
  59.6 17.1 %shard_map.114 = (bf16[3,512,384]{2,1,0:T(8,128)(2,1)}, f32[8,128]{1,0:T(8,128)}) custom-call(s32[8]{0:T(128)} %valid_count.1, s32[8]{0:T(128)} %block_reset.1, f32[8]{0:T(128)} %block_weight.1, bf16[1024,1536]{1,0:T(8,128)(2,1)} %bitcast.8, bf16[768,384]{1,0:T(8,128)(2,1)} %bitcast.9, bf16[3,1536,384]{2,1,0:T(8,128)(2,1)} %bitcast.6, f32[1,128]{1,0:T(1,128)} %bitcast.10, ...), custom_call_target="tpu_custom_call" | custom-call | tf_op jit(solution)/shard_map/pallas_call | solution.py:492
  76.7 0.0 copy-done
  76.8 0.0 copy-start.1
  76.8 1.3 %copy-done.1 = bf16[3,512,384]{2,1,0:T(8,128)(2,1)S(1)} copy-done((bf16[3,512,384]{2,1,0:T(8,128)(2,1)S(1)}, bf16[3,512,384]{2,1,0:T(8,128)(2,1)}, u32[]{:S(2)}) %copy-start.1) | copy-done | bytes 1179672
  78.0 0.0 copy-start.2
  78.0 0.7 copy-done.2
  78.7 14.5 %shard_map.115 = (bf16[128,1536]{1,0:T(8,128)(2,1)S(1)}, f32[8,128]{1,0:T(8,128)S(1)}) custom-call(bf16[3,512,384]{2,1,0:T(8,128)(2,1)S(1)} %copy-done.1, bf16[3,1536,384]{2,1,0:T(8,128)(2,1)S(1)} %bitcast.7, f32[8,128]{1,0:T(8,128)S(1)} %copy-done.2), custom_call_target="tpu_custom_call" | custom-call | tf_op jit(solution)/shard_map/pallas_call | solution.py:642
  93.3 0.5 slice.3
  94.4 0.7 copy.13
Async XLA Ops:
  59.6 17.1 %copy-start = (bf16[3,16,96,384]{3,2,1,0:T(8,128)(2,1)S(1)}, bf16[3,16,96,384]{3,2,1,0:T(8,128)(2,1)}, u32[]{:S(2)}) copy-start(bf16[3,16,96,384]{3,2,1,0:T(8,128)(2,1)} %get-tuple-element.11) | copy-start | bytes 10616836
  76.8 1.3 %copy-start.1 = (bf16[3,512,384]{2,1,0:T(8,128)(2,1)S(1)}, bf16[3,512,384]{2,1,0:T(8,128)(2,1)}, u32[]{:S(2)}) copy-start(bf16[3,512,384]{2,1,0:T(8,128)(2,1)} %get-tuple-element.12.back) | copy-start | bytes 3538948
  78.0 0.7 copy-start.2

commit v3 on v2

--- a/solution.py
+++ b/solution.py
@@ -103,24 +103,22 @@
 
     own_slot = 2 * (1 + y) + c
     their_slot = 2 * (2 - y) + c
-    halo_slot = 6 * (1 - y) + c
-    their_halo = 6 * y + c
-    has_halo = jnp.where(y == 1, z, nz - 1 - z) > 0
-    has_their_halo = jnp.where(y == 0, z, nz - 1 - z) > 0
-    give_halo = jnp.where(y == 0, z, nz - 1 - z) > 0
-    halo_to = (g, jnp.where(y == 0, t - QUAD, t + QUAD))
-    halo_to_slot = 6 * (1 - y) + c
+    upper = y == 1
 
     def send_tok(src, slot, i, device):
         return remote(src, tokb.at[slot], tok_send.at[i], tok_recv.at[slot], device)
 
     own_y = send_tok(tok, own_slot, 0, ynbr)
     own_c = send_tok(tok, own_slot, 1, cnbr)
-    own_z = send_tok(tok, halo_to_slot, 2, halo_to)
-    halo_y = send_tok(tokb.at[halo_slot], halo_slot, 3, ynbr)
-    halo_c = send_tok(tokb.at[halo_slot], halo_slot, 4, cnbr)
-    their_c = send_tok(tokb.at[their_slot], their_slot, 5, cnbr)
-    their_halo_c = send_tok(tokb.at[their_halo], their_halo, 6, cnbr)
+    own_z = send_tok(tok, c, 2, (g, t + QUAD))
+    their_c = send_tok(tokb.at[their_slot], their_slot, 3, cnbr)
+    their_z = remote(
+        tokb.at[their_slot], tokb.at[6 + c], tok_send.at[4], tok_recv.at[6 + c], (g, t - QUAD)
+    )
+    before_y = send_tok(tokb.at[c], c, 5, ynbr)
+    before_c = send_tok(tokb.at[c], c, 6, cnbr)
+    after_y = send_tok(tokb.at[6 + c], 6 + c, 7, ynbr)
+    after_c = send_tok(tokb.at[6 + c], 6 + c, 8, cnbr)
     tok_own = pltpu.make_async_copy(tok, tokb.at[own_slot], tok_local.at[0])
 
     def tok_wait(slot):
@@ -153,7 +151,7 @@
         inject_own(w).start()
         if w == ORDER[0]:
 
-            @pl.when(give_halo)
+            @pl.when(upper & has_up)
             def _():
                 own_z.start()
 
@@ -183,24 +181,56 @@
         for m in range(QUAD):
             tgt_before(m).start()
 
-    def relay_halo():
-        @pl.when(has_halo)
-        def _():
-            tok_wait(halo_slot)
-            halo_y.start()
-            halo_c.start()
-
     def relay_theirs():
         tok_wait(their_slot)
         their_c.start()
 
-    def relay_their_halo():
-        @pl.when(has_their_halo)
-        def _():
-            tok_wait(their_halo)
-            their_halo_c.start()
-
-    tasks = [relay_halo, relay_theirs, relay_their_halo]
+        @pl.when(upper & has_dn)
+        def _():
+            their_z.start()
+
+    def relay_before():
+        @pl.when(has_dn)
+        def _():
+            tok_wait(c)
+            before_c.start()
+
+            @pl.when(upper)
+            def _():
+                before_y.start()
+
+    def relay_after():
+        @pl.when(has_up)
+        def _():
+            tok_wait(6 + c)
+            after_c.start()
+
+            @pl.when(upper)
+            def _():
+                after_y.start()
+
+    def early():
+        relay_theirs()
+
+        @pl.when(upper)
+        def _():
+            relay_before()
+
+    def middle():
+        @pl.when(upper)
+        def _():
+            relay_after()
+
+        @pl.when(jnp.logical_not(upper))
+        def _():
+            relay_before()
+
+    def late():
+        @pl.when(jnp.logical_not(upper))
+        def _():
+            relay_after()
+
+    tasks = [early, middle, late]
     for s in range(1, nz):
         for w in ORDER:
 
@@ -266,18 +296,29 @@
     own_c.wait_send()
     their_c.wait_send()
 
-    @pl.when(give_halo)
+    @pl.when(upper & has_up)
     def _():
         own_z.wait_send()
 
-    @pl.when(has_halo)
-    def _():
-        halo_y.wait_send()
-        halo_c.wait_send()
-
-    @pl.when(has_their_halo)
-    def _():
-        their_halo_c.wait_send()
+    @pl.when(upper & has_dn)
+    def _():
+        their_z.wait_send()
+
+    @pl.when(has_dn)
+    def _():
+        before_c.wait_send()
+
+        @pl.when(upper)
+        def _():
+            before_y.wait_send()
+
+    @pl.when(has_up)
+    def _():
+        after_c.wait_send()
+
+        @pl.when(upper)
+        def _():
+            after_y.wait_send()
 
     for d in range(1, QUAD):
         tgt_quad(d).wait_send()
@@ -337,7 +378,7 @@
         scratch_shapes=[
             dma((3, QUAD)), dma((3, QUAD - 1)), dma((3,)),
             dma((3, nz)), dma((3, nz)), dma((3, nz)), dma((3, nz)), dma((3, nz)), dma((3, nz)),
-            dma((8,)), dma((7,)), dma((1,)), dma((6,)), dma((7,)), dma((1,)),
+            dma((8,)), dma((9,)), dma((1,)), dma((6,)), dma((7,)), dma((1,)),
         ],
         compiler_params=pltpu.CompilerParams(collective_id=0, has_side_effects=True),
     )(tokens, target, w_query, w_key, w_value)
@@ -511,7 +552,7 @@
             pltpu.VMEM((heads, 2 * block, head_size), f32),
             pltpu.SemaphoreType.DMA((8,)),
         ],
-        compiler_params=pltpu.CompilerParams(vmem_limit_bytes=56 * 1024 * 1024),
+        compiler_params=pltpu.CompilerParams(vmem_limit_bytes=58 * 1024 * 1024),
     )(
         valid_count, block_reset, block_weight, tok, tgt, w,
         q_gain.reshape(1, head_size), k_gain.reshape(1, head_size),
@@ -522,8 +563,8 @@
 
 
 def share_kernel(
-    n, back, w_hbm, loss, out, loss_out, w, part, cbuf, ysend, yrecv, lbuf,
-    w_sem, c_send, c_recv, y_send, y_recv, l_send, l_recv,
+    n, back_hbm, w_hbm, loss_hbm, out, loss_out, back, w, part, cbuf, ysend, yrecv, lbuf,
+    w_sem, in_sem, c_send, c_recv, y_send, y_recv, l_send, l_recv,
 ):
     g, t = lax.axis_index("groups"), lax.axis_index("tm")
     k = t % QUAD
@@ -538,8 +579,12 @@
         span = slice(i * step, (i + 1) * step)
         return pltpu.make_async_copy(w_hbm.at[:, span], w.at[:, span], w_sem.at[i])
 
+    back_copy = pltpu.make_async_copy(back_hbm, back, in_sem.at[0])
+    loss_copy = pltpu.make_async_copy(loss_hbm, lbuf.at[t], in_sem.at[1])
+    back_copy.start()
     for i in range(CHUNKS):
         w_copy(i).start()
+    loss_copy.start()
 
     barrier = pltpu.get_barrier_semaphore()
 
@@ -581,19 +626,20 @@
 
     def to_all(d):
         return pltpu.make_async_remote_copy(
-            src_ref=loss, dst_ref=lbuf.at[t], send_sem=l_send.at[d],
+            src_ref=lbuf.at[t], dst_ref=lbuf.at[t], send_sem=l_send.at[d],
             recv_sem=l_recv.at[t], device_id=(g, (t + d) % n), device_id_type=MESH,
         )
 
     def from_all(d):
         source = (t + d) % n
         return pltpu.make_async_remote_copy(
-            src_ref=loss, dst_ref=lbuf.at[source], send_sem=l_send.at[d],
+            src_ref=lbuf.at[source], dst_ref=lbuf.at[source], send_sem=l_send.at[d],
             recv_sem=l_recv.at[source], device_id=(g, source), device_id_type=MESH,
         )
 
+    back_copy.wait()
     compute(0)
-    lbuf[t] = loss[...]
+    loss_copy.wait()
     pl.semaphore_wait(barrier, n - 1)
     to_core(0, 1 - y).start()
     to_core(0, y).start()
@@ -645,20 +691,21 @@
             jax.ShapeDtypeStruct((rows, depth), bf16),
             jax.ShapeDtypeStruct((8, 128), jnp.float32),
         ),
-        in_specs=[vmem, pl.BlockSpec(memory_space=pl.ANY), vmem],
+        in_specs=[pl.BlockSpec(memory_space=pl.ANY)] * 3,
         out_specs=(vmem, vmem),
         scratch_shapes=[
+            pltpu.VMEM(back.shape, bf16),
             pltpu.VMEM(w.shape, bf16),
             pltpu.VMEM((CHUNKS, QUAD, rows, step), bf16),
             pltpu.VMEM((CHUNKS, 2, rows, step), bf16),
             pltpu.VMEM((CHUNKS, rows, step), bf16),
             pltpu.VMEM((CHUNKS, rows, step), bf16),
             pltpu.VMEM((n, 8, 128), jnp.float32),
-            dma((CHUNKS,)), dma((CHUNKS, 2)), dma((CHUNKS, 2)), dma((CHUNKS,)), dma((CHUNKS,)),
+            dma((CHUNKS,)), dma((2,)), dma((CHUNKS, 2)), dma((CHUNKS, 2)), dma((CHUNKS,)), dma((CHUNKS,)),
             dma((n,)), dma((n,)),
         ],
         compiler_params=pltpu.CompilerParams(
-            collective_id=1, has_side_effects=True, vmem_limit_bytes=48 * 1024 * 1024),
+            collective_id=1, has_side_effects=True, vmem_limit_bytes=58 * 1024 * 1024),
     )(back, w, loss)
 
 

time: 96.5 us -> 95.6 us (level)
    pallas_call x1, Pallas kernels: 59 us -> 56.1 us  [gather(): pl.pallas_call(functools.partial(gather_kernel, nz), out_shape=(jax.Shape...]
    pallas_call x1, Pallas kernels: 14.5 us -> 17.1 us  [share(): pl.pallas_call(functools.partial(share_kernel, n), out_shape=(jax.ShapeDt...]
    unnamed x7 -> x1, local copies, waits for them, and re-layouts: 2.7 us -> 1.77 us
where the time goes in v3:
time: 95.6 us; the launch traced here: 95.4 us
  Pallas kernels  90 us (94%)
  local copies, waits for them, and re-layouts  2.95 us (3%)
  between operations  2.44 us (3%)
    pallas_call x1, Pallas kernels, gather(): pl.pallas_call(functools.partial(gather_kernel, nz), out_shape=(jax.Shape...  56.1 us
    pallas_call x1, Pallas kernels, share(): pl.pallas_call(functools.partial(share_kernel, n), out_shape=(jax.ShapeDt...  17.1 us
    pallas_call x1, Pallas kernels, layer(): pl.pallas_call(functools.partial(layer_kernel, heads, head_size, block),...  16.8 us

profile of v3, /device:TPU:0, one launch (start us, length us, event | category | flops | bytes accessed | tf_op | source)
XLA Modules:
  0.0 95.4 jit_solution(1938393199246131875)
XLA Ops:
  0.6 56.1 %shard_map.113 = (bf16[8,128,1536]{2,1,0:T(8,128)(2,1)}, bf16[6,128,384]{2,1,0:T(8,128)(2,1)}, bf16[3,16,96,384]{3,2,1,0:T(8,128)(2,1)}) custom-call(bf16[128,1536]{1,0:T(8,128)(2,1)} %tok.1, bf16[128,1536]{1,0:T(8,128)(2,1)} %tgt.1, bf16[96,1536]{1,0:T(8,128)(2,1)} %wq.1, bf16[96,1536]{1,0:T(8,128)(2,1)} %wk.1, bf16[96,1536]{1,0:T(8,128)(2,1)} %wv.1), custom_call_target="tpu_custom_call" | custom-call | tf_op jit(solution)/shard_map/pallas_call | solution.py:369
  56.8 16.8 %shard_map.114 = (bf16[3,512,384]{2,1,0:T(8,128)(2,1)}, f32[8,128]{1,0:T(8,128)}) custom-call(s32[8]{0:T(128)} %valid_count.1, s32[8]{0:T(128)} %block_reset.1, f32[8]{0:T(128)} %block_weight.1, bf16[1024,1536]{1,0:T(8,128)(2,1)} %bitcast.8, bf16[768,384]{1,0:T(8,128)(2,1)} %bitcast.9, bf16[3,1536,384]{2,1,0:T(8,128)(2,1)} %bitcast.6, f32[1,128]{1,0:T(1,128)} %bitcast.10, ...), custom_call_target="tpu_custom_call" | custom-call | tf_op jit(solution)/shard_map/pallas_call | solution.py:533
  73.6 17.1 %shard_map.115 = (bf16[128,1536]{1,0:T(8,128)(2,1)}, f32[8,128]{1,0:T(8,128)}) custom-call(bf16[3,512,384]{2,1,0:T(8,128)(2,1)} %get-tuple-element.12.back_hbm, bf16[3,1536,384]{2,1,0:T(8,128)(2,1)} %bitcast.7, f32[8,128]{1,0:T(8,128)} %get-tuple-element.13.loss_hbm), custom_call_target="tpu_custom_call" | custom-call | tf_op jit(solution)/shard_map/pallas_call | solution.py:688
  90.6 1.2 %slice.3 = f32[1,1]{1,0:T(1,128)} slice(f32[8,128]{1,0:T(8,128)} %get-tuple-element.15), slice={[0:1], [0:1]} | slice | bytes 8 | tf_op jit(solution)/shard_map/slice | solution.py:733
  92.5 1.8 %copy.13 = bf16[128,1536]{1,0:T(8,128)(2,1)} copy(bf16[128,1536]{1,0:T(8,128)(2,1)} %get-tuple-element.18) | data formatting | bytes 786432

commit v4 on v3

--- a/solution.py
+++ b/solution.py
@@ -155,23 +155,21 @@
             def _():
                 own_z.start()
 
+        for d in range(1, QUAD):
+            injected(w, d).wait_recv()
+        inject_own(w).wait()
+
+        @pl.when(has_up)
+        def _():
+            go_up(w, z).start()
+
+        @pl.when(has_dn)
+        def _():
+            go_dn(w, z).start()
+
     own_c.start()
     tok_own.start()
     tgt_own.start()
-
-    for w in ORDER:
-        for d in range(1, QUAD):
-            injected(w, d).wait_recv()
-        inject_own(w).wait()
-
-        @pl.when(has_up)
-        def _():
-            go_up(w, z).start()
-
-        @pl.when(has_dn)
-        def _():
-            go_dn(w, z).start()
-
     own_y.start()
     for d in range(1, QUAD):
         tgt_quad(d).start()
@@ -644,16 +642,16 @@
     to_core(0, 1 - y).start()
     to_core(0, y).start()
 
+    @pl.loop(1, n)
+    def _(d):
+        to_all(d).start()
+
     for i in range(1, CHUNKS):
         compute(i)
         to_core(i, 1 - y).start()
         to_core(i, y).start()
         pass_on(i - 1)
     pass_on(CHUNKS - 1)
-
-    @pl.loop(1, n)
-    def _(d):
-        to_all(d).start()
 
     @pl.loop(1, n)
     def _(d):

time: 95.6 us -> 99.2 us (1.038)
  Pallas kernels: 90 us -> 93.6 us
    pallas_call x1, Pallas kernels: 56.1 us -> 60.1 us  [gather(): pl.pallas_call(functools.partial(gather_kernel, nz), out_shape=(jax.Shape...]
where the time goes in v4:
time: 99.2 us; the launch traced here: 98.9 us
  Pallas kernels  93.6 us (94%)
  local copies, waits for them, and re-layouts  2.95 us (3%)
  between operations  2.44 us (2%)
    pallas_call x1, Pallas kernels, gather(): pl.pallas_call(functools.partial(gather_kernel, nz), out_shape=(jax.Shape...  60.1 us
    pallas_call x1, Pallas kernels, layer(): pl.pallas_call(functools.partial(layer_kernel, heads, head_size, block),...  16.8 us
    pallas_call x1, Pallas kernels, share(): pl.pallas_call(functools.partial(share_kernel, n), out_shape=(jax.ShapeDt...  16.7 us

profile of v4, /device:TPU:0, one launch (start us, length us, event | category | flops | bytes accessed | tf_op | source)
XLA Modules:
  0.0 98.9 jit_solution(11347183196033052457)
XLA Ops:
  0.6 60.1 %shard_map.113 = (bf16[8,128,1536]{2,1,0:T(8,128)(2,1)}, bf16[6,128,384]{2,1,0:T(8,128)(2,1)}, bf16[3,16,96,384]{3,2,1,0:T(8,128)(2,1)}) custom-call(bf16[128,1536]{1,0:T(8,128)(2,1)} %tok.1, bf16[128,1536]{1,0:T(8,128)(2,1)} %tgt.1, bf16[96,1536]{1,0:T(8,128)(2,1)} %wq.1, bf16[96,1536]{1,0:T(8,128)(2,1)} %wk.1, bf16[96,1536]{1,0:T(8,128)(2,1)} %wv.1), custom_call_target="tpu_custom_call" | custom-call | tf_op jit(solution)/shard_map/pallas_call | solution.py:367
  60.7 16.8 %shard_map.114 = (bf16[3,512,384]{2,1,0:T(8,128)(2,1)}, f32[8,128]{1,0:T(8,128)}) custom-call(s32[8]{0:T(128)} %valid_count.1, s32[8]{0:T(128)} %block_reset.1, f32[8]{0:T(128)} %block_weight.1, bf16[1024,1536]{1,0:T(8,128)(2,1)} %bitcast.8, bf16[768,384]{1,0:T(8,128)(2,1)} %bitcast.9, bf16[3,1536,384]{2,1,0:T(8,128)(2,1)} %bitcast.6, f32[1,128]{1,0:T(1,128)} %bitcast.10, ...), custom_call_target="tpu_custom_call" | custom-call | tf_op jit(solution)/shard_map/pallas_call | solution.py:531
  77.5 16.7 %shard_map.115 = (bf16[128,1536]{1,0:T(8,128)(2,1)}, f32[8,128]{1,0:T(8,128)}) custom-call(bf16[3,512,384]{2,1,0:T(8,128)(2,1)} %get-tuple-element.12.back_hbm, bf16[3,1536,384]{2,1,0:T(8,128)(2,1)} %bitcast.7, f32[8,128]{1,0:T(8,128)} %get-tuple-element.13.loss_hbm), custom_call_target="tpu_custom_call" | custom-call | tf_op jit(solution)/shard_map/pallas_call | solution.py:686
  94.2 1.2 %slice.3 = f32[1,1]{1,0:T(1,128)} slice(f32[8,128]{1,0:T(8,128)} %get-tuple-element.15), slice={[0:1], [0:1]} | slice | bytes 8 | tf_op jit(solution)/shard_map/slice | solution.py:731
  96.0 1.8 %copy.13 = bf16[128,1536]{1,0:T(8,128)(2,1)} copy(bf16[128,1536]{1,0:T(8,128)(2,1)} %get-tuple-element.18) | data formatting | bytes 786432
